TPU v7x, 32 devices: a whole 2x2x4 slice. The times are simulated.
32 devices in a mesh: tm: 16 (over z, y, x), space: 2 (over core).
Axes of the slice: x: 2, y: 2, z: 4, core: 2. Of those that a mesh axis runs over, the one named last changes fastest.
Arguments:
- image_gradient: bfloat16 [32, 128, 3, 4096], P('tm', 'space'), may hold values from -0.375 to 0.375
- residual: bfloat16 [32, 128, 4096], P('tm', 'space'), may hold values from -6 to 6
- phase: float32 [32], P('tm'), may hold values from 0 to 1
- counts: int32 [128], P('space'), may hold values from 512 to 4096
- owner: int32 [128, 1], P('space'), may hold values from 0 to 1, as said below
Outputs:
- hessian_blocks: float32 [32, 192, 576], P('tm', 'space')
- gradient_blocks: float32 [32, 192, 24], P('tm', 'space')
Inputs may be any that keep to these rules, and one draw needn't show every extreme that they name: Among the 64 bricks of each aligned block at most 48 share an owner, and one owner takes exactly 48 bricks of every block.
All inputs are finite; a program needn't handle non-finite values.
Results may differ from a plain program's by a relative error of at most 0.0029.
Values sent between devices are 32-bit elements; how exact they have to be, the bound alone decides.
No kernel may reach another device: no remote copies, remote signals or barrier semaphores. Data moves between devices by JAX's collectives and lax.ppermute only.
A program may use at most 64 MiB of HBM per device.

v0:
```python
import jax
import jax.numpy as jnp
from jax import lax
from jax.sharding import PartitionSpec as P

EDGE = 16


def shifted(block, axis, distance):
    devices = range(lax.axis_size(axis))
    route = [(i - distance, i) for i in devices if i - distance in devices]
    return lax.ppermute(block, axis, route)


def spline_weights(phase):
    return jnp.stack(
        [
            (1.0 - phase) ** 3 / 6.0,
            (3.0 * phase**3 - 6.0 * phase**2 + 4.0) / 6.0,
            (-3.0 * phase**3 + 3.0 * phase**2 + 3.0 * phase + 1.0) / 6.0,
            phase**3 / 6.0,
        ],
        axis=-1,
    )


def shape_table(edge):
    voxel = jnp.arange(edge * edge * edge, dtype=jnp.int32)
    first = ((voxel // (edge * edge)).astype(jnp.float32) + 0.5) / edge
    second = ((voxel // edge % edge).astype(jnp.float32) + 0.5) / edge
    third = ((voxel % edge).astype(jnp.float32) + 0.5) / edge
    rows = []
    for node in range(8):
        along_first = first if node >> 2 & 1 else 1.0 - first
        along_second = second if node >> 1 & 1 else 1.0 - second
        along_third = third if node & 1 else 1.0 - third
        rows.append(along_first * along_second * along_third)
    return jnp.stack(rows, axis=0)


def per_device(image_gradient, residual, phase, counts, owner):
    step_count, brick_count, comp_count, voxel_count = image_gradient.shape
    dof_count = 8 * comp_count
    patch_width = dof_count * dof_count
    column_count = patch_width + dof_count
    first_step = lax.axis_index("tm") * step_count
    overall_step_count = lax.axis_size("tm") * step_count
    space_count = lax.axis_size("space")
    capacity = 3 * brick_count // (2 * space_count)
    valid_mask = lax.broadcasted_iota(jnp.int32, (brick_count, voxel_count), 1) < counts[:, None]
    shapes = shape_table(EDGE)

    def per_step(pair):
        grads, resid = pair
        product = shapes[None, :, None, :] * grads.astype(jnp.float32)[:, None, :, :]
        sens = product.reshape(brick_count, dof_count, voxel_count).astype(jnp.bfloat16)
        masked = jnp.where(valid_mask[:, None, :], sens, jnp.zeros((), jnp.bfloat16))
        hessian = jnp.einsum("bdv,bev->bde", masked, masked, preferred_element_type=jnp.float32)
        gradient = jnp.einsum("bdv,bv->bd", masked, resid, preferred_element_type=jnp.float32)
        return jnp.concatenate([hessian.reshape(brick_count, patch_width), gradient], axis=1)

    patch_contents = lax.map(per_step, (image_gradient, residual))
    weights = spline_weights(phase)
    global_step = first_step + jnp.arange(step_count, dtype=jnp.int32)
    target = jnp.clip(
        global_step[:, None] - 1 + jnp.arange(4, dtype=jnp.int32)[None, :],
        0,
        overall_step_count - 1,
    )
    local_slot = target - first_step + 1
    hits_table = (
        local_slot[:, :, None] == jnp.arange(step_count + 3, dtype=jnp.int32)[None, None, :]
    ).astype(jnp.float32)
    basis_lookup_grid = jnp.sum(weights[:, :, None] * hits_table, axis=1)
    is_hessian_column = (jnp.arange(column_count, dtype=jnp.int32) < patch_width)[None, None, :]
    multiplier = jnp.where(
        is_hessian_column,
        (basis_lookup_grid * basis_lookup_grid)[:, :, None],
        basis_lookup_grid[:, :, None],
    )
    owner_flat = owner[:, 0]
    owner_hits = (owner_flat[:, None] == jnp.arange(space_count, dtype=jnp.int32)[None, :]).astype(
        jnp.int32
    )
    earlier = jnp.cumsum(owner_hits, axis=0) - owner_hits
    brick_rank = jnp.sum(earlier * owner_hits, axis=1)
    destination = owner_flat * capacity + brick_rank
    slot_match = (
        destination[:, None] == jnp.arange(space_count * capacity, dtype=jnp.int32)[None, :]
    )
    source_brick = jnp.sum(
        jnp.where(slot_match, jnp.arange(brick_count, dtype=jnp.int32)[:, None], 0), axis=0
    )
    slot_filled = jnp.any(slot_match, axis=0)
    packed = multiplier[0][:, None, :] * patch_contents[0][None]
    packed = packed + multiplier[1][:, None, :] * patch_contents[1][None]
    from_before = shifted(packed[step_count + 1 :], "tm", 1)
    behind = shifted(packed[:1], "tm", -1)
    own_part = packed[1 : step_count + 1]
    own_part = own_part.at[:2].add(from_before)
    picked = jnp.take(own_part.at[step_count - 1 :].add(behind), source_brick, axis=1)
    placed = jnp.where(slot_filled[None, :, None], picked, jnp.zeros((), jnp.float32))
    result = lax.all_to_all(placed, "space", split_axis=1, concat_axis=1, tiled=True)
    return (result[:, :, :patch_width], result[:, :, patch_width:])


def solution(mesh):
    in_specs = (
        P("tm", "space", None, None),
        P("tm", "space", None),
        P("tm"),
        P("space"),
        P("space", None),
    )
    out_specs = (P("tm", "space", None), P("tm", "space", None))
    return jax.shard_map(
        per_device, mesh=mesh, in_specs=in_specs, out_specs=out_specs, check_vma=False
    )
```

profile of v0, /device:TPU:24, one launch (start us, length us, event | category | flops | bytes accessed | tf_op | source)
XLA Modules:
  0.0 131.7 jit_solution(10147643976305642716)
XLA Ops:
  1.3 102.2 %while.14 = (s32[]{:T(128)}, f32[2,64,600]{1,2,0:T(8,128)}, f32[8,4096]{1,0:T(8,128)S(1)}, bf16[2,64,3,4096]{3,1,2,0:T(8,128)(2,1)}, bf16[2,64,4096]{2,1,0:T(8,128)(2,1)}, /*index=5*/s32[64]{0:T(128)}, s32[]{:T(128)}) while((s32[]{:T(128)}, f32[2,64,600]{1,2,0:T(8,128)}, f32[8,4096]{1,0:T(8,128)S(1)}, ...), condition=%wide.region_6.7_spmd.clone, body=%wide.region_5.6_spmd.clone.sunk | while | flops 334534144 | bytes 58191368 | solution.py:62
  1.3 1.8 %bitcast_convert_fusion.2 = f32[64,3,4096]{2,0,1:T(8,128)S(1)} fusion(bf16[2,64,3,4096]{3,1,2,0:T(8,128)(2,1)} %get-tuple-element.176, s32[]{:T(128)S(6)} %copy.47), kind=kLoop, calls=%fused_computation.9.clone.1 | loop fusion | flops 786432 | bytes 4718596 | tf_op jit(solution)/shard_map/while/body/eval_jaxpr/convert_element_type | solution.py:55
  3.1 0.9 mul.344
  4.0 1.2 mul.345
  5.3 0.2 iota_compare_fusion.6
  5.5 6.0 %fusion.46 = bf16[64,24,4096]{2,0,1:T(8,128)(2,1)} fusion(f32[64,3,4096]{2,0,1:T(8,128)S(1)} %bitcast_convert_fusion.2, f32[24,4096]{1,0:T(8,128)S(1)} %mul.345, pred[64,4096]{1,0:T(8,128)(4,1)S(1)} %iota_compare_fusion.6), kind=kLoop, calls=%fused_computation.4.clone.1 | loop fusion | flops 18874368 | bytes 16384000 | tf_op jit(solution)/shard_map/while/body/eval_jaxpr/jit(_where)/select_n | solution.py:57
  11.6 13.3 %fusion.47 = f32[64,1,24]{2,1,0:T(1,128)S(1)} fusion(bf16[64,24,4096]{2,0,1:T(8,128)(2,1)} %fusion.46, bf16[64,4096,1]{1,0,2:T(8,128)(2,1)S(1)} %dynamic-slice_bitcast_fusion.2), kind=kOutput, calls=%fused_computation.5.clone.1 | convolution fusion | flops 12582912 | bytes 13113344 | tf_op jit(solution)/shard_map/while/body/eval_jaxpr/bdv,bv->bd/dot_general | solution.py:59
  25.0 26.2 %fusion.48 = f32[64,24,24]{2,1,0:T(8,128)S(1)} fusion(bf16[64,24,4096]{2,0,1:T(8,128)(2,1)} %fusion.46), kind=kOutput, calls=%fused_computation.7.clone.1 | convolution fusion | flops 301989888 | bytes 12730368 | tf_op jit(solution)/shard_map/while/body/eval_jaxpr/bdv,bev->bde/dot_general | solution.py:58
  51.2 0.3 copy.43
  51.6 0.8 copy-done.4
  52.4 1.8 %bitcast_convert_fusion.2 = f32[64,3,4096]{2,0,1:T(8,128)S(1)} fusion(bf16[2,64,3,4096]{3,1,2,0:T(8,128)(2,1)} %get-tuple-element.176, s32[]{:T(128)S(6)} %copy.47), kind=kLoop, calls=%fused_computation.9.clone.1 | loop fusion | flops 786432 | bytes 4718596 | tf_op jit(solution)/shard_map/while/body/eval_jaxpr/convert_element_type | solution.py:55
  54.2 0.9 mul.344
  55.1 1.2 mul.345
  56.4 0.2 iota_compare_fusion.6
  56.6 6.0 %fusion.46 = bf16[64,24,4096]{2,0,1:T(8,128)(2,1)} fusion(f32[64,3,4096]{2,0,1:T(8,128)S(1)} %bitcast_convert_fusion.2, f32[24,4096]{1,0:T(8,128)S(1)} %mul.345, pred[64,4096]{1,0:T(8,128)(4,1)S(1)} %iota_compare_fusion.6), kind=kLoop, calls=%fused_computation.4.clone.1 | loop fusion | flops 18874368 | bytes 16384000 | tf_op jit(solution)/shard_map/while/body/eval_jaxpr/jit(_where)/select_n | solution.py:57
  62.7 13.3 %fusion.47 = f32[64,1,24]{2,1,0:T(1,128)S(1)} fusion(bf16[64,24,4096]{2,0,1:T(8,128)(2,1)} %fusion.46, bf16[64,4096,1]{1,0,2:T(8,128)(2,1)S(1)} %dynamic-slice_bitcast_fusion.2), kind=kOutput, calls=%fused_computation.5.clone.1 | convolution fusion | flops 12582912 | bytes 13113344 | tf_op jit(solution)/shard_map/while/body/eval_jaxpr/bdv,bv->bd/dot_general | solution.py:59
  76.1 26.2 %fusion.48 = f32[64,24,24]{2,1,0:T(8,128)S(1)} fusion(bf16[64,24,4096]{2,0,1:T(8,128)(2,1)} %fusion.46), kind=kOutput, calls=%fused_computation.7.clone.1 | convolution fusion | flops 301989888 | bytes 12730368 | tf_op jit(solution)/shard_map/while/body/eval_jaxpr/bdv,bev->bde/dot_general | solution.py:58
  102.3 0.3 copy.43
  102.7 0.8 copy-done.4
  103.5 1.1 slice_bitcast_fusion.1
  105.6 3.4 %collective-permute-start = (f32[2,64,600]{2,0,1:T(2,128)S(1)}, f32[2,64,600]{2,0,1:T(2,128)S(1)}, u32[]{:S(2)}, u32[]{:S(2)}) collective-permute-start(f32[2,64,600]{2,0,1:T(2,128)S(1)} %slice.85), channel_id=1, source_target_pairs={{0,2},{2,4},{4,6},{6,8},{8,10},{10,12},{12,14},{14,16},{16,18},{18... | collective-permute-start | bytes 921608 | tf_op jit(solution)/shard_map/ppermute | solution.py:12
  109.2 4.2 %collective-permute-start.1 = (f32[1,64,600]{2,0,1:T(1,128)S(1)}, f32[1,64,600]{2,0,1:T(1,128)S(1)}, u32[]{:S(2)}, u32[]{:S(2)}) collective-permute-start(f32[1,64,600]{2,0,1:T(1,128)S(1)} %slice.87), channel_id=1, source_target_pairs={{2,0},{4,2},{6,4},{8,6},{10,8},{12,10},{14,12},{16,14},{18,16},{20... | collective-permute-start | bytes 460808 | tf_op jit(solution)/shard_map/ppermute | solution.py:12
  114.0 4.9 %collective-permute-done = f32[2,64,600]{2,0,1:T(2,128)S(1)} collective-permute-done((f32[2,64,600]{2,0,1:T(2,128)S(1)}, f32[2,64,600]{2,0,1:T(2,128)S(1)}, u32[]{:S(2)}, u32[]{:S(2)}) %collective-permute-start) | collective-permute-done | bytes 307232 | tf_op jit(solution)/shard_map/ppermute | solution.py:12
  118.9 0.3 slice_add_fusion
  119.1 2.3 %collective-permute-done.1 = f32[1,64,600]{2,0,1:T(1,128)S(1)} collective-permute-done((f32[1,64,600]{2,0,1:T(1,128)S(1)}, f32[1,64,600]{2,0,1:T(1,128)S(1)}, u32[]{:S(2)}, u32[]{:S(2)}) %collective-permute-start.1) | collective-permute-done | bytes 153632 | tf_op jit(solution)/shard_map/ppermute | solution.py:12
  121.5 0.3 slice_add_fusion.1
  121.7 2.7 %scatter-add.4 = f32[2,64,600]{2,0,1:T(2,128)S(1)} dynamic-update-slice(f32[2,64,600]{2,0,1:T(2,128)S(1)} %slice_add_fusion, f32[1,64,600]{2,0,1:T(1,128)S(1)} %slice_add_fusion.1, s32[]{:T(128)} %constant.202.clone.1, s32[]{:T(128)} %constant.192.clone.1, s32[]{:T(128)} %constant.192.clone.1) | dynamic-update-slice | bytes 307204 | tf_op jit(solution)/shard_map/scatter-add | solution.py:101
  124.5 1.1 gather_fusion
  125.6 0.4 select_bitcast_fusion
  126.0 4.1 %all_to_all.5 = f32[2,96,600]{2,0,1:T(2,128)S(1)} all-to-all(f32[2,96,600]{2,0,1:T(2,128)S(1)} %select_bitcast_fusion), channel_id=1, replica_groups=mesh['tm'=16,'space'=2] {'space'}, dimensions={1} | all-to-all | bytes 921600 | tf_op jit(solution)/shard_map/all_to_all | solution.py:103
  130.1 0.8 copy.24
  131.0 0.7 copy.25
  (63 shorter events, 2.7 us)
Async XLA Ops:
  1.3 103.5 %copy-start.7 = (f32[2]{0:T(128)S(1)}, f32[2]{0:T(128)}, u32[]{:S(2)}) copy-start(f32[2]{0:T(128)} %param.15) | copy-start | bytes 28
  1.3 112.1 %copy-start.6 = (s32[64,1]{0,1:T(1,128)S(1)}, s32[64,1]{0,1:T(1,128)}, u32[]{:S(2)}) copy-start(s32[64,1]{0,1:T(1,128)} %param.17) | copy-start | bytes 772
  1.3 1.8 %copy-start.1 = (f32[8,4096]{1,0:T(8,128)}, f32[8,4096]{1,0:T(8,128)S(1)}, u32[]{:S(2)}) copy-start(f32[8,4096]{1,0:T(8,128)S(1)} %get-tuple-element.175) | copy-start | bytes 393220 | tf_op jit(solution)/shard_map/while
  1.3 4.0 %copy-start.5 = (s32[64]{0:T(128)S(1)}, s32[64]{0:T(128)}, u32[]{:S(2)}) copy-start(s32[64]{0:T(128)} %get-tuple-element.178) | copy-start | bytes 772 | tf_op jit(solution)/shard_map/while
  5.5 6.1 %copy-start = (bf16[2,64,4096]{2,1,0:T(8,128)(2,1)S(1)}, bf16[2,64,4096]{2,1,0:T(8,128)(2,1)}, u32[]{:S(2)}) copy-start(bf16[2,64,4096]{2,1,0:T(8,128)(2,1)} %get-tuple-element.177) | copy-start | bytes 3145732 | tf_op jit(solution)/shard_map/while
  25.0 26.5 %copy-start.3 = (f32[2,64,600]{1,2,0:T(8,128)S(1)}, f32[2,64,600]{1,2,0:T(8,128)}, u32[]{:S(2)}) copy-start(f32[2,64,600]{1,2,0:T(8,128)} %get-tuple-element.167) | copy-start | bytes 921604 | tf_op jit(solution)/shard_map/while
  25.0 27.4 %copy-start.2 = (f32[8,4096]{1,0:T(8,128)S(1)}, f32[8,4096]{1,0:T(8,128)}, u32[]{:S(2)}) copy-start(f32[8,4096]{1,0:T(8,128)} %copy-done.1) | copy-start | bytes 393220 | tf_op jit(solution)/shard_map/while
  51.6 0.9 copy-start.4
  52.4 1.8 %copy-start.1 = (f32[8,4096]{1,0:T(8,128)}, f32[8,4096]{1,0:T(8,128)S(1)}, u32[]{:S(2)}) copy-start(f32[8,4096]{1,0:T(8,128)S(1)} %get-tuple-element.175) | copy-start | bytes 393220 | tf_op jit(solution)/shard_map/while
  52.4 4.0 %copy-start.5 = (s32[64]{0:T(128)S(1)}, s32[64]{0:T(128)}, u32[]{:S(2)}) copy-start(s32[64]{0:T(128)} %get-tuple-element.178) | copy-start | bytes 772 | tf_op jit(solution)/shard_map/while
  56.6 6.1 %copy-start = (bf16[2,64,4096]{2,1,0:T(8,128)(2,1)S(1)}, bf16[2,64,4096]{2,1,0:T(8,128)(2,1)}, u32[]{:S(2)}) copy-start(bf16[2,64,4096]{2,1,0:T(8,128)(2,1)} %get-tuple-element.177) | copy-start | bytes 3145732 | tf_op jit(solution)/shard_map/while
  76.1 26.5 %copy-start.3 = (f32[2,64,600]{1,2,0:T(8,128)S(1)}, f32[2,64,600]{1,2,0:T(8,128)}, u32[]{:S(2)}) copy-start(f32[2,64,600]{1,2,0:T(8,128)} %get-tuple-element.167) | copy-start | bytes 921604 | tf_op jit(solution)/shard_map/while
  76.1 27.4 %copy-start.2 = (f32[8,4096]{1,0:T(8,128)S(1)}, f32[8,4096]{1,0:T(8,128)}, u32[]{:S(2)}) copy-start(f32[8,4096]{1,0:T(8,128)} %copy-done.1) | copy-start | bytes 393220 | tf_op jit(solution)/shard_map/while
  102.7 0.9 copy-start.4
  105.6 13.2 %collective-permute-start = (f32[2,64,600]{2,0,1:T(2,128)S(1)}, f32[2,64,600]{2,0,1:T(2,128)S(1)}, u32[]{:S(2)}, u32[]{:S(2)}) collective-permute-start(f32[2,64,600]{2,0,1:T(2,128)S(1)} %slice.85), channel_id=1, source_target_pairs={{0,2},{2,4},{4,6},{6,8},{8,10},{10,12},{12,14},{14,16},{16,18},{18... | collective-permute-start | bytes 921608 | tf_op jit(solution)/shard_map/ppermute | solution.py:12
  109.2 12.3 %collective-permute-start.1 = (f32[1,64,600]{2,0,1:T(1,128)S(1)}, f32[1,64,600]{2,0,1:T(1,128)S(1)}, u32[]{:S(2)}, u32[]{:S(2)}) collective-permute-start(f32[1,64,600]{2,0,1:T(1,128)S(1)} %slice.87), channel_id=1, source_target_pairs={{2,0},{4,2},{6,4},{8,6},{10,8},{12,10},{14,12},{16,14},{18,16},{20... | collective-permute-start | bytes 460808 | tf_op jit(solution)/shard_map/ppermute | solution.py:12
where the time goes:
time: 134 us; the launch traced here: 132 us
  matrix products  79.1 us (59%)
  other arithmetic  18.4 us (14%)
  local copies, waits for them, and re-layouts  14.3 us (11%)
  starting transfers between devices  7.64 us (6%)
  waiting for transfers between devices  7.17 us (5%)
  blocking collectives  4.11 us (3%)
    dot_general x2, matrix products, per_step(): jnp.einsum('bdv,bev->bde', masked, masked, preferred_element_type=jnp.flo...  52.5 us
    dot_general x2, matrix products, per_step(): jnp.einsum('bdv,bv->bd', masked, resid, preferred_element_type=jnp.float32)  26.7 us
    select_n x2, other arithmetic, per_step(): jnp.where(valid_mask[:, None, :], sens, jnp.zeros((), jnp.bfloat16))  12.1 us
    ppermute x2, starting transfers between devices, shifted(): return lax.ppermute(block, axis, route)  7.64 us
    ppermute x2, waiting for transfers between devices, shifted(): return lax.ppermute(block, axis, route)  7.17 us
    mul x4, local copies, waits for them, and re-layouts, per_step(): shapes[None, :, None, :] * grads.astype(jnp.float32)[:, None, :, :]  4.25 us
    all_to_all x1, blocking collectives, per_device(): lax.all_to_all(placed, 'space', split_axis=1, concat_axis=1, tiled=True)  4.11 us
    convert_element_type x2, other arithmetic, per_step(): grads.astype(jnp.float32)[:, None, :, :]  3.61 us
  transfers between devices with their start and end apart: 2, of which 2 were waited for; matrix products, arithmetic and copies ran while one was open for 1% of the time, Pallas kernels for 0%

commit v1 on v0

v1 whole, which is shorter than its diff:
```python
import functools
import math

import ml_dtypes
import numpy as np
import jax
import jax.numpy as jnp
from jax import lax
from jax.experimental import pallas as pl
from jax.experimental.pallas import tpu as pltpu
from jax.sharding import PartitionSpec as P

LANES = 128
QUADS = 27
NODES = 8
SLOT = 32
WIDTH = 2 * LANES
GRAD_AT = 6 * SLOT
DEST_AT = WIDTH - 1
LOW_AT = 64
BF16 = jnp.bfloat16
F32 = jnp.float32


def component_pairs(comps):
    return [(c, e) for c in range(comps) for e in range(c, comps)]


@functools.cache
def voxel_tables(voxels):
    edge = round(voxels ** (1 / 3))
    at = (np.arange(edge) + 0.5) / edge
    lines = np.stack([1 - at, at])
    quads = np.stack([(1 - at) ** 2, at * (1 - at), at * at])
    shapes = np.einsum("ai,bj,ck->abcijk", lines, lines, lines).reshape(NODES, voxels)
    squares = np.einsum("ai,bj,ck->abcijk", quads, quads, quads).reshape(QUADS, voxels)
    scale = (1 + np.floor(128 * np.modf(np.arange(voxels) * 0.6180339887498949)[0]) / 128).reshape(1, voxels)
    rows = np.concatenate([squares / scale, shapes])
    high = rows.astype(ml_dtypes.bfloat16)
    low = (rows - high.astype(np.float64)).astype(ml_dtypes.bfloat16)
    table = np.zeros((voxels, LANES), ml_dtypes.bfloat16)
    table[:, : QUADS + NODES] = high.T
    table[:, LOW_AT : LOW_AT + QUADS + NODES] = low.T
    return table, scale.astype(ml_dtypes.bfloat16)


@functools.cache
def expansion_tables(comps):
    dofs = NODES * comps
    pairs = component_pairs(comps)
    hessian = np.zeros((WIDTH, dofs * dofs), ml_dtypes.bfloat16)
    gradient = np.zeros((dofs, WIDTH), ml_dtypes.bfloat16)
    for d in range(dofs):
        a, c = divmod(d, comps)
        gradient[d, GRAD_AT + NODES * c + a] = 1
        for f in range(dofs):
            b, e = divmod(f, comps)
            quad = sum(((a >> k & 1) + (b >> k & 1)) * 3**k for k in range(3))
            hessian[SLOT * pairs.index((min(c, e), max(c, e))) + quad, d * dofs + f] = 1
    return hessian, gradient


def spline_weights(phase):
    return [
        (1.0 - phase) ** 3 / 6.0,
        (3.0 * phase**3 - 6.0 * phase**2 + 4.0) / 6.0,
        (-3.0 * phase**3 + 3.0 * phase**2 + 3.0 * phase + 1.0) / 6.0,
        phase**3 / 6.0,
    ]


def column(row):
    n = row.shape[1]
    eye = lax.broadcasted_iota(jnp.int32, (n, n), 0) == lax.broadcasted_iota(jnp.int32, (n, n), 1)
    return jnp.sum(jnp.where(eye, jnp.broadcast_to(row, (n, n)), 0.0), axis=1, keepdims=True)


def moments_kernel(
    chunk,
    capacity,
    grads_hbm,
    resid_hbm,
    counts_hbm,
    owner_hbm,
    phase_hbm,
    table_hbm,
    scale_hbm,
    own_ref,
    send_a_ref,
    send_b_ref,
    grads,
    resid,
    counts_ref,
    owner_ref,
    phase_ref,
    table,
    scale,
    products_a,
    products_b,
    moments,
    small_sems,
    sems,
):
    steps, comps, bricks, voxels = grads.shape
    pairs = component_pairs(comps)
    groups = len(pairs) + 2 * comps
    small = [
        pltpu.make_async_copy(src, dst, small_sems.at[i])
        for i, (src, dst) in enumerate(
            [
                (counts_hbm, counts_ref),
                (owner_hbm, owner_ref),
                (phase_hbm, phase_ref),
                (scale_hbm, scale),
                (table_hbm, table),
            ]
        )
    ]
    parts = []
    for s in range(steps):
        for b in range(0, bricks, chunk):
            i = 2 * len(parts)
            rows = pl.ds(b, chunk)
            parts.append(
                (
                    s,
                    b,
                    pltpu.make_async_copy(grads_hbm.at[s, :, rows], grads.at[s, :, rows], sems.at[i]),
                    pltpu.make_async_copy(resid_hbm.at[s, rows], resid.at[s, rows], sems.at[i + 1]),
                )
            )
    for copy in small:
        copy.start()
    for _, _, grads_copy, resid_copy in parts:
        grads_copy.start()
        resid_copy.start()

    lane = lax.broadcasted_iota(jnp.int32, (1, LANES), 1)

    def fill(s, b, products):
        rows = slice(b, b + chunk)
        limit = jnp.broadcast_to(counts[rows], (chunk, LANES)).astype(jnp.int16)
        zero = jnp.zeros((), BF16)
        for at in range(0, voxels, LANES):
            cols = slice(at, at + LANES)
            voxel = lax.broadcasted_iota(jnp.int16, (chunk, LANES), 1) + jnp.int16(at)
            valid = voxel < limit
            scale_here = jnp.where(valid, jnp.broadcast_to(scale[:, cols], (chunk, LANES)), zero)
            resid_here = jnp.where(valid, resid[s, rows, cols], zero).astype(F32)
            g = [grads[s, c, rows, cols] for c in range(comps)]
            scaled = [x * scale_here for x in g]
            blocks = [scaled[c] * g[e] for c, e in pairs]
            for c in range(comps):
                exact = g[c].astype(F32) * resid_here
                high = exact.astype(BF16)
                blocks += [high, (exact - high.astype(F32)).astype(BF16)]
            for i, block in enumerate(blocks):
                products[i * chunk : (i + 1) * chunk, cols] = block

    def reduce(s, b, products):
        sums = jnp.dot(products[...], table[...], preferred_element_type=F32)
        halves = [jnp.zeros((chunk, LANES), F32) for _ in range(2)]
        whole = [sums[i * chunk : (i + 1) * chunk] for i in range(len(pairs))]
        for c in range(comps):
            i = len(pairs) + 2 * c
            whole.append(sums[i * chunk : (i + 1) * chunk] + sums[(i + 1) * chunk : (i + 2) * chunk])
        for i, block in enumerate(whole):
            block = block + pltpu.roll(block, LANES - LOW_AT, 1)
            if i < len(pairs):
                source, goal, span = 0, SLOT * i, QUADS
            else:
                source, goal, span = QUADS, GRAD_AT + NODES * (i - len(pairs)), NODES
            half, goal = divmod(goal, LANES)
            shift = (goal - source) % LANES
            if shift:
                block = pltpu.roll(block, shift, 1)
            keep = (lane >= goal) & (lane < goal + span)
            halves[half] = jnp.where(keep, block, halves[half])
        for half in range(2):
            moments[s, b : b + chunk, half * LANES : (half + 1) * LANES] = halves[half]

    for copy in small[:4]:
        copy.wait()
    counts = column(counts_ref[...].astype(F32)).astype(jnp.int32)
    owner_row = owner_ref[...].astype(F32)
    owner_col = column(owner_row)
    square = (bricks, bricks)
    earlier = lax.broadcasted_iota(jnp.int32, square, 1) < lax.broadcasted_iota(jnp.int32, square, 0)
    same = (owner_col == owner_row) & earlier
    rank = jnp.sum(jnp.where(same, 1.0, 0.0), axis=1, keepdims=True)
    destination = owner_col * capacity + rank

    buffers = (products_a, products_b)
    for i, (s, b, grads_copy, resid_copy) in enumerate(parts):
        grads_copy.wait()
        resid_copy.wait()
        if i == 1:
            small[4].wait()
        fill(s, b, buffers[i % 2])
        if i:
            before = parts[i - 1]
            reduce(before[0], before[1], buffers[(i - 1) % 2])
    if len(parts) == 1:
        small[4].wait()
    reduce(parts[-1][0], parts[-1][1], buffers[(len(parts) - 1) % 2])

    place = lax.axis_index("tm")
    places = lax.axis_size("tm")
    first_step = place * steps
    weights = [spline_weights(phase_ref[:, s : s + 1]) for s in range(steps)]

    def coefficient(position):
        total = [jnp.zeros((bricks, LANES), F32) for _ in range(2)]
        for s in range(steps):
            basis = jnp.zeros((1, 1), F32)
            for j in range(4):
                reach = s - 1 + j
                if position not in (reach, max(reach, 0), min(reach, steps - 1)):
                    continue
                goal = jnp.clip(first_step + reach, 0, places * steps - 1) - first_step
                basis = basis + jnp.where(goal == position, weights[s][j], 0.0)
            squared = basis * basis
            factors = [
                jnp.broadcast_to(squared, (1, LANES)),
                jnp.where(lane < GRAD_AT - LANES, squared, basis),
            ]
            for half in range(2):
                total[half] += factors[half] * moments[s, :, half * LANES : (half + 1) * LANES]
        return total

    odd = place % 2 == 1
    empty = [jnp.zeros((bricks, LANES), F32) for _ in range(2)]
    above = [coefficient(steps + k) if k < 2 else empty for k in range(steps)]
    below = [coefficient(-1) if k == steps - 1 else empty for k in range(steps)]
    for k in range(steps):
        mine = coefficient(k)
        mine[1] = jnp.where(lane == DEST_AT - LANES, destination, mine[1])
        for half in range(2):
            cols = slice(half * LANES, (half + 1) * LANES)
            own_ref[k, :, cols] = mine[half]
            send_a_ref[k, :, cols] = jnp.where(odd, below[k][half], above[k][half])
            send_b_ref[k, :, cols] = jnp.where(odd, above[k][half], below[k][half])


def split3(x):
    high = x.astype(BF16)
    rest = x - high.astype(F32)
    middle = rest.astype(BF16)
    return high, middle, (rest - middle.astype(F32)).astype(BF16)


def expand_kernel(capacity, count, *refs):
    blocks = refs[:count]
    hessian_table, gradient_table, hessian_ref, gradient_ref = refs[count:]
    steps, bricks, _ = blocks[0].shape
    slots = hessian_ref.shape[1]
    me = lax.axis_index("space")
    slot = lax.broadcasted_iota(jnp.int32, (bricks, slots), 1).astype(F32)
    picks = []
    for distance, block in enumerate(blocks):
        source = (me + count - distance) % count
        rank = block[0, :, DEST_AT : DEST_AT + 1] - (me * capacity).astype(F32)
        mine = (rank >= 0.0) & (rank < capacity)
        goal = jnp.where(mine, rank + (source * capacity).astype(F32), -1.0)
        picks.append(jnp.where(slot == goal, 1.0, 0.0))
    pick = jnp.concatenate(picks, axis=0).astype(BF16)
    for k in range(steps):
        values = jnp.concatenate([block[k] for block in blocks], axis=0)
        hessian = gradient = None
        for part in split3(values):
            placed = lax.dot_general(
                pick, part, (((0,), (0,)), ((), ())), preferred_element_type=F32
            ).astype(BF16)
            wide = jnp.dot(placed, hessian_table[...], preferred_element_type=F32)
            thin = lax.dot_general(
                gradient_table[...], placed, (((1,), (1,)), ((), ())), preferred_element_type=F32
            )
            hessian = wide if hessian is None else hessian + wide
            gradient = thin if gradient is None else gradient + thin
        hessian_ref[k] = hessian
        gradient_ref[k] = gradient


def per_device(image_gradient, residual, phase, counts, owner):
    steps, bricks, comps, voxels = image_gradient.shape
    spaces = lax.axis_size("space")
    places = lax.axis_size("tm")
    capacity = 3 * bricks // (2 * spaces)
    dofs = NODES * comps
    chunk = math.gcd(bricks, 32)
    groups = len(component_pairs(comps)) + 2 * comps
    table, scale = voxel_tables(voxels)
    block = (steps, bricks, WIDTH)
    chunks = steps * bricks // chunk
    any_space = pl.BlockSpec(memory_space=pl.ANY)
    own, send_a, send_b = pl.pallas_call(
        functools.partial(moments_kernel, chunk, capacity),
        in_specs=[any_space] * 7,
        out_shape=[pltpu.VMEM(block, F32)] * 3,
        scratch_shapes=[
            pltpu.VMEM((steps, comps, bricks, voxels), BF16),
            pltpu.VMEM((steps, bricks, voxels), BF16),
            pltpu.VMEM((1, bricks), jnp.int32),
            pltpu.VMEM((1, bricks), jnp.int32),
            pltpu.VMEM((1, steps), F32),
            pltpu.VMEM((voxels, LANES), BF16),
            pltpu.VMEM((1, voxels), BF16),
            pltpu.VMEM((groups * chunk, voxels), BF16),
            pltpu.VMEM((groups * chunk, voxels), BF16),
            pltpu.VMEM(block, F32),
            pltpu.SemaphoreType.DMA((5,)),
            pltpu.SemaphoreType.DMA((2 * chunks,)),
        ],
        compiler_params=pltpu.CompilerParams(vmem_limit_bytes=32 << 20),
        name="moments",
    )(
        jnp.transpose(image_gradient, (0, 2, 1, 3)),
        residual,
        counts.reshape(1, bricks),
        owner.reshape(1, bricks),
        phase.reshape(1, steps),
        jnp.asarray(table),
        jnp.asarray(scale),
    )

    def exchange(values, start):
        lower = range(start, places - 1, 2)
        route = [(i, i + 1) for i in lower] + [(i + 1, i) for i in lower]
        return lax.ppermute(values, "tm", route) if route else jnp.zeros_like(values)

    total = own + exchange(send_a, 0) + exchange(send_b, 1)
    blocks = [total]
    for distance in range(1, spaces):
        route = [(i, (i + distance) % spaces) for i in range(spaces)]
        blocks.append(lax.ppermute(total, "space", route))
    hessian_table, gradient_table = expansion_tables(comps)
    hessian, gradient = pl.pallas_call(
        functools.partial(expand_kernel, capacity, spaces),
        out_shape=[
            jax.ShapeDtypeStruct((steps, spaces * capacity, dofs * dofs), F32),
            jax.ShapeDtypeStruct((steps, dofs, spaces * capacity), F32),
        ],
        compiler_params=pltpu.CompilerParams(vmem_limit_bytes=16 << 20),
        name="expand",
    )(*blocks, jnp.asarray(hessian_table), jnp.asarray(gradient_table))
    return hessian, jnp.transpose(gradient, (0, 2, 1))


def solution(mesh):
    in_specs = (
        P("tm", "space", None, None),
        P("tm", "space", None),
        P("tm"),
        P("space"),
        P("space", None),
    )
    out_specs = (P("tm", "space", None), P("tm", "space", None))
    return jax.shard_map(
        per_device, mesh=mesh, in_specs=in_specs, out_specs=out_specs, check_vma=False
    )
```

time: 134 us -> 31.5 us (0.24)
  the two profiles are of different devices: /device:TPU:24 before, /device:TPU:9 now
where the time goes in v1:
time: 31.5 us; the launch traced here: 31.2 us
  Pallas kernels  11.6 us (37%)
  local copies, waits for them, and re-layouts  7.02 us (22%)
  starting transfers between devices  6.44 us (20%)
  waiting for transfers between devices  5.48 us (17%)
  between operations  0.67 us (2%)
    pallas_call x1, Pallas kernels, per_device(): pl.pallas_call(functools.partial(moments_kernel, chunk, capacity), in_spe...  9.66 us
    unnamed x18, local copies, waits for them, and re-layouts  7.02 us
    ppermute x2, waiting for transfers between devices, exchange(): lax.ppermute(values, 'tm', route)  4.5 us
    ppermute x2, starting transfers between devices, exchange(): lax.ppermute(values, 'tm', route)  4.27 us
    ppermute x1, starting transfers between devices, per_device(): blocks.append(lax.ppermute(total, 'space', route))  2.17 us
    pallas_call x1, Pallas kernels, per_device(): pl.pallas_call(functools.partial(expand_kernel, capacity, spaces), out_sh...  1.91 us
    ppermute x1, waiting for transfers between devices, per_device(): blocks.append(lax.ppermute(total, 'space', route))  0.99 us
  transfers between devices with their start and end apart: 3, of which 3 were waited for; matrix products, arithmetic and copies ran while one was open for 0% of the time, Pallas kernels for 0%

profile of v1, /device:TPU:9, one launch (start us, length us, event | category | flops | bytes accessed | tf_op | source)
XLA Modules:
  0.0 31.2 jit_solution(2809910209048146781)
XLA Ops:
  0.6 0.0 copy-start
  0.6 1.9 %copy-done = bf16[2,64,3,4096]{3,1,2,0:T(8,128)(2,1)S(1)} copy-done((bf16[2,64,3,4096]{3,1,2,0:T(8,128)(2,1)S(1)}, bf16[2,64,3,4096]{3,1,2,0:T(8,128)(2,1)}, u32[]{:S(2)}) %copy-start) | copy-done | bytes 3145752
  2.5 0.0 copy-start.1
  2.5 1.2 %copy-done.1 = bf16[2,64,4096]{2,1,0:T(8,128)(2,1)S(1)} copy-done((bf16[2,64,4096]{2,1,0:T(8,128)(2,1)S(1)}, bf16[2,64,4096]{2,1,0:T(8,128)(2,1)}, u32[]{:S(2)}) %copy-start.1) | copy-done | bytes 1048600
  3.7 0.0 copy-start.2
  3.7 1.2 %copy-done.2 = bf16[4096,128]{1,0:T(8,128)(2,1)S(1)} copy-done((bf16[4096,128]{1,0:T(8,128)(2,1)S(1)}, bf16[4096,128]{1,0:T(8,128)(2,1)}, u32[]{:S(2)}) %copy-start.2) | copy-done | bytes 1048600
  5.0 0.0 copy-start.4
  5.0 0.7 %copy-done.4 = bf16[1,4096]{1,0:T(2,128)(2,1)S(1)} copy-done((bf16[1,4096]{1,0:T(2,128)(2,1)S(1)}, bf16[1,4096]{1,0:T(2,128)(2,1)}, u32[]{:S(2)}) %copy-start.4) | copy-done | bytes 8216
  5.7 0.0 copy-start.6
  5.7 0.7 %copy-done.6 = s32[64]{0:T(128)S(1)} copy-done((s32[64]{0:T(128)S(1)}, s32[64]{0:T(128)}, u32[]{:S(2)}) %copy-start.6) | copy-done | bytes 280
  6.3 0.0 copy-start.7
  6.3 0.7 %copy-done.7 = s32[64,1]{0,1:T(1,128)S(1)} copy-done((s32[64,1]{0,1:T(1,128)S(1)}, s32[64,1]{0,1:T(1,128)}, u32[]{:S(2)}) %copy-start.7) | copy-done | bytes 280
  7.0 0.0 copy-start.8
  7.0 0.7 %copy-done.8 = f32[2]{0:T(128)S(1)} copy-done((f32[2]{0:T(128)S(1)}, f32[2]{0:T(128)}, u32[]{:S(2)}) %copy-start.8) | copy-done | bytes 32
  7.7 0.0 copy-start.3
  7.7 0.0 copy-start.5
  7.7 9.7 %moments.1 = (f32[2,64,256]{2,1,0:T(8,128)S(1)}, f32[2,64,256]{2,1,0:T(8,128)S(1)}, f32[2,64,256]{2,1,0:T(8,128)S(1)}) custom-call(bf16[2,3,64,4096]{3,2,1,0:T(8,128)(2,1)S(1)} %bitcast.5, bf16[2,64,4096]{2,1,0:T(8,128)(2,1)S(1)} %copy-done.1, s32[1,64]{1,0:T(1,128)S(1)} %bitcast.6, s32[1,64]{1,0:T(1,128)S(1)} %bitcast.7, f32[1,2]{1,0:T(1,128)S(1)} %bitcast.8, ...), custom_call_target="tpu_custom_call" | custom-call | tf_op jit(solution)/shard_map/moments/pallas_call | solution.py:296
  17.3 1.3 %collective-permute-start = (f32[2,64,256]{2,1,0:T(8,128)S(1)}, f32[2,64,256]{2,1,0:T(8,128)S(1)}, u32[]{:S(2)}, u32[]{:S(2)}) collective-permute-start(f32[2,64,256]{2,1,0:T(8,128)S(1)} %get-tuple-element.8), channel_id=1, source_target_pairs={{0,2},{4,6},{8,10},{12,14},{16,18},{20,22},{24,26},{28,30},{2,0},{... | collective-permute-start | bytes 393224 | tf_op jit(solution)/shard_map/ppermute | solution.py:329
  18.6 3.0 %collective-permute-start.1 = (f32[2,64,256]{2,1,0:T(8,128)S(1)}, f32[2,64,256]{2,1,0:T(8,128)S(1)}, u32[]{:S(2)}, u32[]{:S(2)}) collective-permute-start(f32[2,64,256]{2,1,0:T(8,128)S(1)} %get-tuple-element.9), channel_id=1, source_target_pairs={{2,4},{6,8},{10,12},{14,16},{18,20},{22,24},{26,28},{4,2},{8,6},{1... | collective-permute-start | bytes 393224 | tf_op jit(solution)/shard_map/ppermute | solution.py:329
  21.6 0.1 collective-permute-done
  21.8 4.4 %collective-permute-done.1 = f32[2,64,256]{2,1,0:T(8,128)S(1)} collective-permute-done((f32[2,64,256]{2,1,0:T(8,128)S(1)}, f32[2,64,256]{2,1,0:T(8,128)S(1)}, u32[]{:S(2)}, u32[]{:S(2)}) %collective-permute-start.1) | collective-permute-done | bytes 131104 | tf_op jit(solution)/shard_map/ppermute | solution.py:329
  26.1 2.2 %collective-permute-start.2 = (f32[2,64,256]{2,1,0:T(8,128)S(1)}, f32[2,64,256]{2,1,0:T(8,128)S(1)}, u32[]{:S(2)}, u32[]{:S(2)}) collective-permute-start(f32[2,64,256]{2,1,0:T(8,128)S(1)} %add_add_fusion.refs_0_), channel_id=1, source_target_pairs={{0,1},{1,0},{2,3},{3,2},{4,5},{5,4},{6,7},{7,6},{8,9},{9,8},{10,11... | collective-permute-start | bytes 393224 | tf_op jit(solution)/shard_map/ppermute | solution.py:335
  28.3 1.0 %collective-permute-done.2.refs_1_ = f32[2,64,256]{2,1,0:T(8,128)S(1)} collective-permute-done((f32[2,64,256]{2,1,0:T(8,128)S(1)}, f32[2,64,256]{2,1,0:T(8,128)S(1)}, u32[]{:S(2)}, u32[]{:S(2)}) %collective-permute-start.2) | collective-permute-done | bytes 131104 | tf_op jit(solution)/shard_map/ppermute | solution.py:335
  29.3 0.0 copy-done.3
  29.3 0.0 copy-done.5
  29.3 1.9 %expand.1 = (f32[2,96,576]{2,1,0:T(8,128)}, f32[2,24,96]{2,1,0:T(8,128)}) custom-call(f32[2,64,256]{2,1,0:T(8,128)S(1)} %add_add_fusion.refs_0_, f32[2,64,256]{2,1,0:T(8,128)S(1)} %collective-permute-done.2.refs_1_, bf16[256,576]{1,0:T(8,128)(2,1)S(1)} %copy-done.3, bf16[24,256]{1,0:T(8,128)(2,1)S(1)} %copy-done.5), custom_call_target="tpu_custom_call" | custom-call | tf_op jit(solution)/shard_map/expand/pallas_call | solution.py:337
  (1 shorter events, 0.0 us)
Async XLA Ops:
  0.6 1.9 %copy-start = (bf16[2,64,3,4096]{3,1,2,0:T(8,128)(2,1)S(1)}, bf16[2,64,3,4096]{3,1,2,0:T(8,128)(2,1)}, u32[]{:S(2)}) copy-start(bf16[2,64,3,4096]{3,1,2,0:T(8,128)(2,1)} %param.9) | copy-start | bytes 9437188
  2.5 1.2 %copy-start.1 = (bf16[2,64,4096]{2,1,0:T(8,128)(2,1)S(1)}, bf16[2,64,4096]{2,1,0:T(8,128)(2,1)}, u32[]{:S(2)}) copy-start(bf16[2,64,4096]{2,1,0:T(8,128)(2,1)} %resid_hbm.1) | copy-start | bytes 3145732
  3.7 1.2 %copy-start.2 = (bf16[4096,128]{1,0:T(8,128)(2,1)S(1)}, bf16[4096,128]{1,0:T(8,128)(2,1)}, u32[]{:S(2)}) copy-start(bf16[4096,128]{1,0:T(8,128)(2,1)} %constant.8.clone.table_hbm) | copy-start | bytes 3145732
  5.0 0.7 %copy-start.4 = (bf16[1,4096]{1,0:T(2,128)(2,1)S(1)}, bf16[1,4096]{1,0:T(2,128)(2,1)}, u32[]{:S(2)}) copy-start(bf16[1,4096]{1,0:T(2,128)(2,1)} %constant.9.clone.scale_hbm) | copy-start | bytes 24580
  5.7 0.7 %copy-start.6 = (s32[64]{0:T(128)S(1)}, s32[64]{0:T(128)}, u32[]{:S(2)}) copy-start(s32[64]{0:T(128)} %param.12) | copy-start | bytes 772
  6.3 0.7 %copy-start.7 = (s32[64,1]{0,1:T(1,128)S(1)}, s32[64,1]{0,1:T(1,128)}, u32[]{:S(2)}) copy-start(s32[64,1]{0,1:T(1,128)} %param.13) | copy-start | bytes 772
  7.0 0.7 %copy-start.8 = (f32[2]{0:T(128)S(1)}, f32[2]{0:T(128)}, u32[]{:S(2)}) copy-start(f32[2]{0:T(128)} %param.11) | copy-start | bytes 28
  7.7 21.6 %copy-start.3 = (bf16[256,576]{1,0:T(8,128)(2,1)S(1)}, bf16[256,576]{1,0:T(8,128)(2,1)}, u32[]{:S(2)}) copy-start(bf16[256,576]{1,0:T(8,128)(2,1)} %constant.10.clone.refs_2_) | copy-start | bytes 884740
  7.7 21.6 %copy-start.5 = (bf16[24,256]{1,0:T(8,128)(2,1)S(1)}, bf16[24,256]{1,0:T(8,128)(2,1)}, u32[]{:S(2)}) copy-start(bf16[24,256]{1,0:T(8,128)(2,1)} %constant.11.clone.refs_3_) | copy-start | bytes 36868
  17.3 4.4 %collective-permute-start = (f32[2,64,256]{2,1,0:T(8,128)S(1)}, f32[2,64,256]{2,1,0:T(8,128)S(1)}, u32[]{:S(2)}, u32[]{:S(2)}) collective-permute-start(f32[2,64,256]{2,1,0:T(8,128)S(1)} %get-tuple-element.8), channel_id=1, source_target_pairs={{0,2},{4,6},{8,10},{12,14},{16,18},{20,22},{24,26},{28,30},{2,0},{... | collective-permute-start | bytes 393224 | tf_op jit(solution)/shard_map/ppermute | solution.py:329
  18.6 7.5 %collective-permute-start.1 = (f32[2,64,256]{2,1,0:T(8,128)S(1)}, f32[2,64,256]{2,1,0:T(8,128)S(1)}, u32[]{:S(2)}, u32[]{:S(2)}) collective-permute-start(f32[2,64,256]{2,1,0:T(8,128)S(1)} %get-tuple-element.9), channel_id=1, source_target_pairs={{2,4},{6,8},{10,12},{14,16},{18,20},{22,24},{26,28},{4,2},{8,6},{1... | collective-permute-start | bytes 393224 | tf_op jit(solution)/shard_map/ppermute | solution.py:329
  26.1 3.2 %collective-permute-start.2 = (f32[2,64,256]{2,1,0:T(8,128)S(1)}, f32[2,64,256]{2,1,0:T(8,128)S(1)}, u32[]{:S(2)}, u32[]{:S(2)}) collective-permute-start(f32[2,64,256]{2,1,0:T(8,128)S(1)} %add_add_fusion.refs_0_), channel_id=1, source_target_pairs={{0,1},{1,0},{2,3},{3,2},{4,5},{5,4},{6,7},{7,6},{8,9},{9,8},{10,11... | collective-permute-start | bytes 393224 | tf_op jit(solution)/shard_map/ppermute | solution.py:335

commit v2 on v1

--- a/solution.py
+++ b/solution.py
@@ -13,11 +13,10 @@
 LANES = 128
 QUADS = 27
 NODES = 8
-SLOT = 32
+PER_HALF = 3
+GRAD_AT = PER_HALF * QUADS
 WIDTH = 2 * LANES
-GRAD_AT = 6 * SLOT
 DEST_AT = WIDTH - 1
-LOW_AT = 64
 BF16 = jnp.bfloat16
 F32 = jnp.float32
 
@@ -35,13 +34,21 @@
     shapes = np.einsum("ai,bj,ck->abcijk", lines, lines, lines).reshape(NODES, voxels)
     squares = np.einsum("ai,bj,ck->abcijk", quads, quads, quads).reshape(QUADS, voxels)
     scale = (1 + np.floor(128 * np.modf(np.arange(voxels) * 0.6180339887498949)[0]) / 128).reshape(1, voxels)
-    rows = np.concatenate([squares / scale, shapes])
-    high = rows.astype(ml_dtypes.bfloat16)
-    low = (rows - high.astype(np.float64)).astype(ml_dtypes.bfloat16)
-    table = np.zeros((voxels, LANES), ml_dtypes.bfloat16)
-    table[:, : QUADS + NODES] = high.T
-    table[:, LOW_AT : LOW_AT + QUADS + NODES] = low.T
-    return table, scale.astype(ml_dtypes.bfloat16)
+    squares = (squares / scale).astype(ml_dtypes.bfloat16)
+    high = shapes.astype(ml_dtypes.bfloat16)
+    low = (shapes - high.astype(np.float64)).astype(ml_dtypes.bfloat16)
+    table = np.zeros((LANES, voxels), ml_dtypes.bfloat16)
+    rows = np.concatenate([squares] * PER_HALF + [high, low] * 2)
+    table[: len(rows)] = rows
+    return np.ascontiguousarray(table.T), np.repeat(scale.astype(ml_dtypes.bfloat16), 16, axis=0)
+
+
+def pair_place(i):
+    return i // PER_HALF, i % PER_HALF * QUADS, QUADS
+
+
+def gradient_place(c):
+    return c % 2, GRAD_AT + c // 2 * 2 * NODES, 2 * NODES
 
 
 @functools.cache
@@ -52,11 +59,13 @@
     gradient = np.zeros((dofs, WIDTH), ml_dtypes.bfloat16)
     for d in range(dofs):
         a, c = divmod(d, comps)
-        gradient[d, GRAD_AT + NODES * c + a] = 1
+        half, at, _ = gradient_place(c)
+        gradient[d, [half * LANES + at + a, half * LANES + at + NODES + a]] = 1
         for f in range(dofs):
             b, e = divmod(f, comps)
             quad = sum(((a >> k & 1) + (b >> k & 1)) * 3**k for k in range(3))
-            hessian[SLOT * pairs.index((min(c, e), max(c, e))) + quad, d * dofs + f] = 1
+            half, at, _ = pair_place(pairs.index((min(c, e), max(c, e))))
+            hessian[half * LANES + at + quad, d * dofs + f] = 1
     return hessian, gradient
 
 
@@ -76,7 +85,6 @@
 
 
 def moments_kernel(
-    chunk,
     capacity,
     grads_hbm,
     resid_hbm,
@@ -97,13 +105,20 @@
     scale,
     products_a,
     products_b,
+    limits,
+    sums,
     moments,
     small_sems,
     sems,
 ):
     steps, comps, bricks, voxels = grads.shape
     pairs = component_pairs(comps)
-    groups = len(pairs) + 2 * comps
+    groups = len(pairs) + comps
+    rows = steps * bricks
+    plane = round(voxels ** (2 / 3))
+    width = products_a.shape[1]
+    buffers = (products_a, products_b)
+    parts = voxels // width
     small = [
         pltpu.make_async_copy(src, dst, small_sems.at[i])
         for i, (src, dst) in enumerate(
@@ -112,76 +127,61 @@
                 (owner_hbm, owner_ref),
                 (phase_hbm, phase_ref),
                 (scale_hbm, scale),
-                (table_hbm, table),
             ]
         )
     ]
-    parts = []
-    for s in range(steps):
-        for b in range(0, bricks, chunk):
-            i = 2 * len(parts)
-            rows = pl.ds(b, chunk)
-            parts.append(
-                (
-                    s,
-                    b,
-                    pltpu.make_async_copy(grads_hbm.at[s, :, rows], grads.at[s, :, rows], sems.at[i]),
-                    pltpu.make_async_copy(resid_hbm.at[s, rows], resid.at[s, rows], sems.at[i + 1]),
-                )
-            )
+
+    def copies(k):
+        cols = pl.ds(pl.multiple_of(k * width, width), width)
+        return (
+            pltpu.make_async_copy(grads_hbm.at[:, :, :, cols], grads.at[:, :, :, cols], sems.at[k, 0]),
+            pltpu.make_async_copy(resid_hbm.at[:, :, cols], resid.at[:, :, cols], sems.at[k, 1]),
+            pltpu.make_async_copy(table_hbm.at[cols], table.at[cols], sems.at[k, 2]),
+        )
+
     for copy in small:
         copy.start()
-    for _, _, grads_copy, resid_copy in parts:
-        grads_copy.start()
-        resid_copy.start()
+    for k in range(parts):
+        for copy in copies(k):
+            copy.start()
 
     lane = lax.broadcasted_iota(jnp.int32, (1, LANES), 1)
-
-    def fill(s, b, products):
-        rows = slice(b, b + chunk)
-        limit = jnp.broadcast_to(counts[rows], (chunk, LANES)).astype(jnp.int16)
-        zero = jnp.zeros((), BF16)
-        for at in range(0, voxels, LANES):
-            cols = slice(at, at + LANES)
-            voxel = lax.broadcasted_iota(jnp.int16, (chunk, LANES), 1) + jnp.int16(at)
-            valid = voxel < limit
-            scale_here = jnp.where(valid, jnp.broadcast_to(scale[:, cols], (chunk, LANES)), zero)
-            resid_here = jnp.where(valid, resid[s, rows, cols], zero).astype(F32)
-            g = [grads[s, c, rows, cols] for c in range(comps)]
-            scaled = [x * scale_here for x in g]
-            blocks = [scaled[c] * g[e] for c, e in pairs]
-            for c in range(comps):
-                exact = g[c].astype(F32) * resid_here
-                high = exact.astype(BF16)
-                blocks += [high, (exact - high.astype(F32)).astype(BF16)]
-            for i, block in enumerate(blocks):
-                products[i * chunk : (i + 1) * chunk, cols] = block
-
-    def reduce(s, b, products):
-        sums = jnp.dot(products[...], table[...], preferred_element_type=F32)
-        halves = [jnp.zeros((chunk, LANES), F32) for _ in range(2)]
-        whole = [sums[i * chunk : (i + 1) * chunk] for i in range(len(pairs))]
-        for c in range(comps):
-            i = len(pairs) + 2 * c
-            whole.append(sums[i * chunk : (i + 1) * chunk] + sums[(i + 1) * chunk : (i + 2) * chunk])
-        for i, block in enumerate(whole):
-            block = block + pltpu.roll(block, LANES - LOW_AT, 1)
-            if i < len(pairs):
-                source, goal, span = 0, SLOT * i, QUADS
-            else:
-                source, goal, span = QUADS, GRAD_AT + NODES * (i - len(pairs)), NODES
-            half, goal = divmod(goal, LANES)
-            shift = (goal - source) % LANES
-            if shift:
-                block = pltpu.roll(block, shift, 1)
-            keep = (lane >= goal) & (lane < goal + span)
-            halves[half] = jnp.where(keep, block, halves[half])
-        for half in range(2):
-            moments[s, b : b + chunk, half * LANES : (half + 1) * LANES] = halves[half]
-
-    for copy in small[:4]:
+    tall = math.gcd(bricks, 16)
+    voxel = lax.broadcasted_iota(jnp.int16, (tall, plane), 1)
+    zero = jnp.zeros((), BF16)
+
+    def fill(k, products):
+        start = k * width
+        for b in range(0, bricks, tall):
+            limit = (limits[b : b + tall] - start).astype(jnp.int16)
+            left = [[None] * comps for _ in range(steps)]
+            for p in range(0, width, plane):
+                cols = pl.ds(pl.multiple_of(start + p, plane), plane)
+                valid = voxel + jnp.int16(p) < limit
+                scale_here = jnp.where(valid, scale[:tall, cols], zero)
+                for s in range(steps):
+                    resid_here = jnp.where(valid, resid[s, b : b + tall, cols], zero).astype(F32)
+                    g = [grads[s, c, b : b + tall, cols] for c in range(comps)]
+                    scaled = [x * scale_here for x in g]
+                    blocks = [scaled[c] * g[e] for c, e in pairs]
+                    for c in range(comps):
+                        exact = g[c].astype(F32) * resid_here
+                        if left[s][c] is not None:
+                            exact = exact + left[s][c]
+                        blocks.append(exact.astype(BF16))
+                        left[s][c] = exact - blocks[-1].astype(F32)
+                    for i, block in enumerate(blocks):
+                        at = i * rows + s * bricks + b
+                        products[at : at + tall, p : p + plane] = block
+
+    def reduce(k, products):
+        cols = pl.ds(pl.multiple_of(k * width, width), width)
+        sums[...] += jnp.dot(products[...], table[cols], preferred_element_type=F32)
+
+    for copy in small:
         copy.wait()
     counts = column(counts_ref[...].astype(F32)).astype(jnp.int32)
+    limits[...] = jnp.broadcast_to(counts, (bricks, plane))
     owner_row = owner_ref[...].astype(F32)
     owner_col = column(owner_row)
     square = (bricks, bricks)
@@ -189,20 +189,24 @@
     same = (owner_col == owner_row) & earlier
     rank = jnp.sum(jnp.where(same, 1.0, 0.0), axis=1, keepdims=True)
     destination = owner_col * capacity + rank
-
-    buffers = (products_a, products_b)
-    for i, (s, b, grads_copy, resid_copy) in enumerate(parts):
-        grads_copy.wait()
-        resid_copy.wait()
-        if i == 1:
-            small[4].wait()
-        fill(s, b, buffers[i % 2])
-        if i:
-            before = parts[i - 1]
-            reduce(before[0], before[1], buffers[(i - 1) % 2])
-    if len(parts) == 1:
-        small[4].wait()
-    reduce(parts[-1][0], parts[-1][1], buffers[(len(parts) - 1) % 2])
+    sums[...] = jnp.zeros_like(sums)
+
+    for k in range(parts):
+        for copy in copies(k):
+            copy.wait()
+    for k in range(parts):
+        fill(k, buffers[k % 2])
+        reduce(k, buffers[k % 2])
+
+    for s in range(steps):
+        halves = [jnp.zeros((bricks, LANES), F32) for _ in range(2)]
+        for i in range(groups):
+            half, goal, span = pair_place(i) if i < len(pairs) else gradient_place(i - len(pairs))
+            keep = (lane >= goal) & (lane < goal + span)
+            at = i * rows + s * bricks
+            halves[half] = jnp.where(keep, sums[at : at + bricks], halves[half])
+        for half in range(2):
+            moments[s, :, half * LANES : (half + 1) * LANES] = halves[half]
 
     place = lax.axis_index("tm")
     places = lax.axis_size("tm")
@@ -220,12 +224,9 @@
                 goal = jnp.clip(first_step + reach, 0, places * steps - 1) - first_step
                 basis = basis + jnp.where(goal == position, weights[s][j], 0.0)
             squared = basis * basis
-            factors = [
-                jnp.broadcast_to(squared, (1, LANES)),
-                jnp.where(lane < GRAD_AT - LANES, squared, basis),
-            ]
+            factor = jnp.where(lane < GRAD_AT, squared, basis)
             for half in range(2):
-                total[half] += factors[half] * moments[s, :, half * LANES : (half + 1) * LANES]
+                total[half] += factor * moments[s, :, half * LANES : (half + 1) * LANES]
         return total
 
     odd = place % 2 == 1
@@ -287,15 +288,15 @@
     places = lax.axis_size("tm")
     capacity = 3 * bricks // (2 * spaces)
     dofs = NODES * comps
-    chunk = math.gcd(bricks, 32)
-    groups = len(component_pairs(comps)) + 2 * comps
+    groups = len(component_pairs(comps)) + comps
+    parts = 2
+    width = voxels // parts
     table, scale = voxel_tables(voxels)
     block = (steps, bricks, WIDTH)
-    chunks = steps * bricks // chunk
-    any_space = pl.BlockSpec(memory_space=pl.ANY)
+    in_hbm = pl.BlockSpec(memory_space=pltpu.HBM)
     own, send_a, send_b = pl.pallas_call(
-        functools.partial(moments_kernel, chunk, capacity),
-        in_specs=[any_space] * 7,
+        functools.partial(moments_kernel, capacity),
+        in_specs=[in_hbm] * 7,
         out_shape=[pltpu.VMEM(block, F32)] * 3,
         scratch_shapes=[
             pltpu.VMEM((steps, comps, bricks, voxels), BF16),
@@ -304,23 +305,30 @@
             pltpu.VMEM((1, bricks), jnp.int32),
             pltpu.VMEM((1, steps), F32),
             pltpu.VMEM((voxels, LANES), BF16),
-            pltpu.VMEM((1, voxels), BF16),
-            pltpu.VMEM((groups * chunk, voxels), BF16),
-            pltpu.VMEM((groups * chunk, voxels), BF16),
+            pltpu.VMEM(scale.shape, BF16),
+            pltpu.VMEM((groups * steps * bricks, width), BF16),
+            pltpu.VMEM((groups * steps * bricks, width), BF16),
+            pltpu.VMEM((bricks, round(voxels ** (2 / 3))), jnp.int32),
+            pltpu.VMEM((groups * steps * bricks, LANES), F32),
             pltpu.VMEM(block, F32),
-            pltpu.SemaphoreType.DMA((5,)),
-            pltpu.SemaphoreType.DMA((2 * chunks,)),
+            pltpu.SemaphoreType.DMA((4,)),
+            pltpu.SemaphoreType.DMA((parts, 3)),
         ],
         compiler_params=pltpu.CompilerParams(vmem_limit_bytes=32 << 20),
         name="moments",
     )(
-        jnp.transpose(image_gradient, (0, 2, 1, 3)),
-        residual,
-        counts.reshape(1, bricks),
-        owner.reshape(1, bricks),
-        phase.reshape(1, steps),
-        jnp.asarray(table),
-        jnp.asarray(scale),
+        *(
+            pltpu.with_memory_space_constraint(x, pltpu.HBM)
+            for x in (
+                jnp.transpose(image_gradient, (0, 2, 1, 3)),
+                residual,
+                counts.reshape(1, bricks),
+                owner.reshape(1, bricks),
+                phase.reshape(1, steps),
+                jnp.asarray(table),
+                jnp.asarray(scale),
+            )
+        )
     )
 
     def exchange(values, start):

time: 31.5 us -> 20.6 us (0.65)
  the two profiles are of different devices: /device:TPU:9 before, /device:TPU:17 now
where the time goes in v2:
time: 20.6 us; the launch traced here: 20.4 us
  Pallas kernels  7.77 us (38%)
  starting transfers between devices  6.44 us (31%)
  waiting for transfers between devices  5.48 us (27%)
  between operations  0.67 us (3%)
    pallas_call x1, Pallas kernels, per_device(): pl.pallas_call(functools.partial(moments_kernel, capacity), in_specs=[in_...  5.87 us
    ppermute x2, waiting for transfers between devices, exchange(): lax.ppermute(values, 'tm', route)  4.5 us
    ppermute x2, starting transfers between devices, exchange(): lax.ppermute(values, 'tm', route)  4.27 us
    ppermute x1, starting transfers between devices, per_device(): blocks.append(lax.ppermute(total, 'space', route))  2.18 us
    pallas_call x1, Pallas kernels, per_device(): pl.pallas_call(functools.partial(expand_kernel, capacity, spaces), out_sh...  1.89 us
    ppermute x1, waiting for transfers between devices, per_device(): blocks.append(lax.ppermute(total, 'space', route))  0.99 us
  transfers between devices with their start and end apart: 3, of which 3 were waited for; matrix products, arithmetic and copies ran while one was open for 0% of the time, Pallas kernels for 0%

profile of v2, /device:TPU:17, one launch (start us, length us, event | category | flops | bytes accessed | tf_op | source)
XLA Modules:
  0.0 20.4 jit_solution(14108128569862744425)
XLA Ops:
  0.6 0.0 copy-start.1
  0.6 0.0 copy-start
  0.7 5.9 %moments.1 = (f32[2,64,256]{2,1,0:T(8,128)S(1)}, f32[2,64,256]{2,1,0:T(8,128)S(1)}, f32[2,64,256]{2,1,0:T(8,128)S(1)}) custom-call(bf16[2,3,64,4096]{3,2,1,0:T(8,128)(2,1)} %bitcast.5, bf16[2,64,4096]{2,1,0:T(8,128)(2,1)} %resid_hbm.1, s32[1,64]{1,0:T(1,128)} %bitcast.6, s32[1,64]{1,0:T(1,128)} %bitcast.7, f32[1,2]{1,0:T(1,128)} %bitcast.8, ...), custom_call_target="tpu_custom_call" | custom-call | tf_op jit(solution)/shard_map/moments/pallas_call | solution.py:297
  6.5 1.3 %collective-permute-start = (f32[2,64,256]{2,1,0:T(8,128)S(1)}, f32[2,64,256]{2,1,0:T(8,128)S(1)}, u32[]{:S(2)}, u32[]{:S(2)}) collective-permute-start(f32[2,64,256]{2,1,0:T(8,128)S(1)} %get-tuple-element.8), channel_id=1, source_target_pairs={{0,2},{4,6},{8,10},{12,14},{16,18},{20,22},{24,26},{28,30},{2,0},{... | collective-permute-start | bytes 393224 | tf_op jit(solution)/shard_map/ppermute | solution.py:337
  7.8 3.0 %collective-permute-start.1 = (f32[2,64,256]{2,1,0:T(8,128)S(1)}, f32[2,64,256]{2,1,0:T(8,128)S(1)}, u32[]{:S(2)}, u32[]{:S(2)}) collective-permute-start(f32[2,64,256]{2,1,0:T(8,128)S(1)} %get-tuple-element.9), channel_id=1, source_target_pairs={{2,4},{6,8},{10,12},{14,16},{18,20},{22,24},{26,28},{4,2},{8,6},{1... | collective-permute-start | bytes 393224 | tf_op jit(solution)/shard_map/ppermute | solution.py:337
  10.8 0.2 collective-permute-done
  11.0 4.3 %collective-permute-done.1 = f32[2,64,256]{2,1,0:T(8,128)S(1)} collective-permute-done((f32[2,64,256]{2,1,0:T(8,128)S(1)}, f32[2,64,256]{2,1,0:T(8,128)S(1)}, u32[]{:S(2)}, u32[]{:S(2)}) %collective-permute-start.1) | collective-permute-done | bytes 131104 | tf_op jit(solution)/shard_map/ppermute | solution.py:337
  15.3 2.2 %collective-permute-start.2 = (f32[2,64,256]{2,1,0:T(8,128)S(1)}, f32[2,64,256]{2,1,0:T(8,128)S(1)}, u32[]{:S(2)}, u32[]{:S(2)}) collective-permute-start(f32[2,64,256]{2,1,0:T(8,128)S(1)} %add_add_fusion.refs_0_), channel_id=1, source_target_pairs={{0,1},{1,0},{2,3},{3,2},{4,5},{5,4},{6,7},{7,6},{8,9},{9,8},{10,11... | collective-permute-start | bytes 393224 | tf_op jit(solution)/shard_map/ppermute | solution.py:343
  17.5 1.0 %collective-permute-done.2.refs_1_ = f32[2,64,256]{2,1,0:T(8,128)S(1)} collective-permute-done((f32[2,64,256]{2,1,0:T(8,128)S(1)}, f32[2,64,256]{2,1,0:T(8,128)S(1)}, u32[]{:S(2)}, u32[]{:S(2)}) %collective-permute-start.2) | collective-permute-done | bytes 131104 | tf_op jit(solution)/shard_map/ppermute | solution.py:343
  18.5 0.0 copy-done.1
  18.5 0.0 copy-done
  18.5 1.9 %expand.1 = (f32[2,96,576]{2,1,0:T(8,128)}, f32[2,24,96]{2,1,0:T(8,128)}) custom-call(f32[2,64,256]{2,1,0:T(8,128)S(1)} %add_add_fusion.refs_0_, f32[2,64,256]{2,1,0:T(8,128)S(1)} %collective-permute-done.2.refs_1_, bf16[256,576]{1,0:T(8,128)(2,1)S(1)} %copy-done, bf16[24,256]{1,0:T(8,128)(2,1)S(1)} %copy-done.1), custom_call_target="tpu_custom_call" | custom-call | tf_op jit(solution)/shard_map/expand/pallas_call | solution.py:345
  (1 shorter events, 0.0 us)
Async XLA Ops:
  0.6 17.9 %copy-start.1 = (bf16[24,256]{1,0:T(8,128)(2,1)S(1)}, bf16[24,256]{1,0:T(8,128)(2,1)}, u32[]{:S(2)}) copy-start(bf16[24,256]{1,0:T(8,128)(2,1)} %constant.11.clone.refs_3_) | copy-start | bytes 36868
  0.6 17.9 %copy-start = (bf16[256,576]{1,0:T(8,128)(2,1)S(1)}, bf16[256,576]{1,0:T(8,128)(2,1)}, u32[]{:S(2)}) copy-start(bf16[256,576]{1,0:T(8,128)(2,1)} %constant.10.clone.refs_2_) | copy-start | bytes 884740
  6.5 4.4 %collective-permute-start = (f32[2,64,256]{2,1,0:T(8,128)S(1)}, f32[2,64,256]{2,1,0:T(8,128)S(1)}, u32[]{:S(2)}, u32[]{:S(2)}) collective-permute-start(f32[2,64,256]{2,1,0:T(8,128)S(1)} %get-tuple-element.8), channel_id=1, source_target_pairs={{0,2},{4,6},{8,10},{12,14},{16,18},{20,22},{24,26},{28,30},{2,0},{... | collective-permute-start | bytes 393224 | tf_op jit(solution)/shard_map/ppermute | solution.py:337
  7.8 7.5 %collective-permute-start.1 = (f32[2,64,256]{2,1,0:T(8,128)S(1)}, f32[2,64,256]{2,1,0:T(8,128)S(1)}, u32[]{:S(2)}, u32[]{:S(2)}) collective-permute-start(f32[2,64,256]{2,1,0:T(8,128)S(1)} %get-tuple-element.9), channel_id=1, source_target_pairs={{2,4},{6,8},{10,12},{14,16},{18,20},{22,24},{26,28},{4,2},{8,6},{1... | collective-permute-start | bytes 393224 | tf_op jit(solution)/shard_map/ppermute | solution.py:337
  15.3 3.2 %collective-permute-start.2 = (f32[2,64,256]{2,1,0:T(8,128)S(1)}, f32[2,64,256]{2,1,0:T(8,128)S(1)}, u32[]{:S(2)}, u32[]{:S(2)}) collective-permute-start(f32[2,64,256]{2,1,0:T(8,128)S(1)} %add_add_fusion.refs_0_), channel_id=1, source_target_pairs={{0,1},{1,0},{2,3},{3,2},{4,5},{5,4},{6,7},{7,6},{8,9},{9,8},{10,11... | collective-permute-start | bytes 393224 | tf_op jit(solution)/shard_map/ppermute | solution.py:343

commit v3 on v2

--- a/solution.py
+++ b/solution.py
@@ -15,8 +15,6 @@
 NODES = 8
 PER_HALF = 3
 GRAD_AT = PER_HALF * QUADS
-WIDTH = 2 * LANES
-DEST_AT = WIDTH - 1
 BF16 = jnp.bfloat16
 F32 = jnp.float32
 
@@ -38,34 +36,68 @@
     high = shapes.astype(ml_dtypes.bfloat16)
     low = (shapes - high.astype(np.float64)).astype(ml_dtypes.bfloat16)
     table = np.zeros((LANES, voxels), ml_dtypes.bfloat16)
-    rows = np.concatenate([squares] * PER_HALF + [high, low] * 2)
+    rows = np.concatenate([squares] * PER_HALF + [high, high, low, low])
     table[: len(rows)] = rows
     return np.ascontiguousarray(table.T), np.repeat(scale.astype(ml_dtypes.bfloat16), 16, axis=0)
 
 
+def voxel_parts(voxels, sixteenths):
+    ends = np.cumsum((0,) + sixteenths) * (voxels // 16)
+    return tuple((int(a), int(b - a)) for a, b in zip(ends, ends[1:]))
+
+
 def pair_place(i):
     return i // PER_HALF, i % PER_HALF * QUADS, QUADS
 
 
 def gradient_place(c):
-    return c % 2, GRAD_AT + c // 2 * 2 * NODES, 2 * NODES
+    return c % 2, GRAD_AT + c // 2 * NODES, NODES
 
 
 @functools.cache
-def expansion_tables(comps):
+def packing(steps, comps):
+    ends = [0, 0]
+    places = [pair_place(i) for i in range(len(component_pairs(comps)))]
+    for half, at, count in places + [gradient_place(c) for c in range(comps)]:
+        ends[half] = max(ends[half], at + count)
+    groups = -(-(steps * sum(ends) + 1) // LANES)
+    free = [[g, 0, LANES - (g == groups - 1)] for g in range(groups)]
+    pieces = []
+    for step, half in sorted(np.ndindex(steps, 2), key=lambda x: -ends[x[1]]):
+        source, left = 0, ends[half]
+        while left:
+            gap = max(free, key=lambda f: (f[1] + left <= f[2], f[1] == 0, f[2] - f[1]))
+            count = min(left, gap[2] - gap[1])
+            pieces.append((step, half, source, gap[0], gap[1], count))
+            gap[1] += count
+            source += count
+            left -= count
+    return groups, tuple(pieces)
+
+
+def packed_lane(pieces, step, half, lane):
+    for s, h, source, group, goal, count in pieces:
+        if (s, h) == (step, half) and source <= lane < source + count:
+            return group * LANES + goal + lane - source
+
+
+@functools.cache
+def expansion_tables(steps, comps):
     dofs = NODES * comps
     pairs = component_pairs(comps)
-    hessian = np.zeros((WIDTH, dofs * dofs), ml_dtypes.bfloat16)
-    gradient = np.zeros((dofs, WIDTH), ml_dtypes.bfloat16)
-    for d in range(dofs):
-        a, c = divmod(d, comps)
-        half, at, _ = gradient_place(c)
-        gradient[d, [half * LANES + at + a, half * LANES + at + NODES + a]] = 1
-        for f in range(dofs):
-            b, e = divmod(f, comps)
-            quad = sum(((a >> k & 1) + (b >> k & 1)) * 3**k for k in range(3))
-            half, at, _ = pair_place(pairs.index((min(c, e), max(c, e))))
-            hessian[half * LANES + at + quad, d * dofs + f] = 1
+    groups, pieces = packing(steps, comps)
+    hessian = np.zeros((steps, groups * LANES, dofs * dofs), ml_dtypes.bfloat16)
+    gradient = np.zeros((steps * dofs, groups * LANES), ml_dtypes.bfloat16)
+    for k in range(steps):
+        for d in range(dofs):
+            a, c = divmod(d, comps)
+            half, at, _ = gradient_place(c)
+            gradient[k * dofs + d, packed_lane(pieces, k, half, at + a)] = 1
+            for f in range(dofs):
+                b, e = divmod(f, comps)
+                quad = sum(((a >> n & 1) + (b >> n & 1)) * 3**n for n in range(3))
+                half, at, _ = pair_place(pairs.index((min(c, e), max(c, e))))
+                hessian[k, packed_lane(pieces, k, half, at + quad), d * dofs + f] = 1
     return hessian, gradient
 
 
@@ -86,6 +118,8 @@
 
 def moments_kernel(
     capacity,
+    parts,
+    ahead,
     grads_hbm,
     resid_hbm,
     counts_hbm,
@@ -116,9 +150,7 @@
     groups = len(pairs) + comps
     rows = steps * bricks
     plane = round(voxels ** (2 / 3))
-    width = products_a.shape[1]
     buffers = (products_a, products_b)
-    parts = voxels // width
     small = [
         pltpu.make_async_copy(src, dst, small_sems.at[i])
         for i, (src, dst) in enumerate(
@@ -132,7 +164,8 @@
     ]
 
     def copies(k):
-        cols = pl.ds(pl.multiple_of(k * width, width), width)
+        start, width = parts[k]
+        cols = pl.ds(start, width)
         return (
             pltpu.make_async_copy(grads_hbm.at[:, :, :, cols], grads.at[:, :, :, cols], sems.at[k, 0]),
             pltpu.make_async_copy(resid_hbm.at[:, :, cols], resid.at[:, :, cols], sems.at[k, 1]),
@@ -141,7 +174,7 @@
 
     for copy in small:
         copy.start()
-    for k in range(parts):
+    for k in range(ahead):
         for copy in copies(k):
             copy.start()
 
@@ -151,12 +184,12 @@
     zero = jnp.zeros((), BF16)
 
     def fill(k, products):
-        start = k * width
+        start, width = parts[k]
         for b in range(0, bricks, tall):
             limit = (limits[b : b + tall] - start).astype(jnp.int16)
             left = [[None] * comps for _ in range(steps)]
             for p in range(0, width, plane):
-                cols = pl.ds(pl.multiple_of(start + p, plane), plane)
+                cols = slice(start + p, start + p + plane)
                 valid = voxel + jnp.int16(p) < limit
                 scale_here = jnp.where(valid, scale[:tall, cols], zero)
                 for s in range(steps):
@@ -175,8 +208,11 @@
                         products[at : at + tall, p : p + plane] = block
 
     def reduce(k, products):
-        cols = pl.ds(pl.multiple_of(k * width, width), width)
-        sums[...] += jnp.dot(products[...], table[cols], preferred_element_type=F32)
+        start, width = parts[k]
+        for at in range(0, groups * rows, groups * rows // 2):
+            here = slice(at, at + groups * rows // 2)
+            part = jnp.dot(products[here, :width], table[start : start + width], preferred_element_type=F32)
+            sums[here] = part if k == 0 else sums[here] + part
 
     for copy in small:
         copy.wait()
@@ -189,24 +225,34 @@
     same = (owner_col == owner_row) & earlier
     rank = jnp.sum(jnp.where(same, 1.0, 0.0), axis=1, keepdims=True)
     destination = owner_col * capacity + rank
-    sums[...] = jnp.zeros_like(sums)
-
-    for k in range(parts):
+
+    for k in range(len(parts)):
         for copy in copies(k):
             copy.wait()
-    for k in range(parts):
+        if k + ahead < len(parts):
+            for copy in copies(k + ahead):
+                copy.start()
         fill(k, buffers[k % 2])
         reduce(k, buffers[k % 2])
 
+    doubled = (comps + 1) // 2 * NODES
     for s in range(steps):
         halves = [jnp.zeros((bricks, LANES), F32) for _ in range(2)]
         for i in range(groups):
-            half, goal, span = pair_place(i) if i < len(pairs) else gradient_place(i - len(pairs))
-            keep = (lane >= goal) & (lane < goal + span)
             at = i * rows + s * bricks
-            halves[half] = jnp.where(keep, sums[at : at + bricks], halves[half])
+            block = sums[at : at + bricks]
+            if i < len(pairs):
+                half, goal, span = pair_place(i)
+                keep = (lane >= goal) & (lane < goal + span)
+            else:
+                half, goal, span = gradient_place(i - len(pairs))
+                keep = (lane >= goal) & (lane < goal + span)
+                keep |= (lane >= goal + doubled) & (lane < goal + doubled + span)
+            halves[half] = jnp.where(keep, block, halves[half])
         for half in range(2):
-            moments[s, :, half * LANES : (half + 1) * LANES] = halves[half]
+            low = pltpu.roll(halves[half], LANES - doubled, 1)
+            whole = halves[half] + jnp.where(lane >= GRAD_AT, low, 0.0)
+            moments[s, :, half * LANES : (half + 1) * LANES] = whole
 
     place = lax.axis_index("tm")
     places = lax.axis_size("tm")
@@ -229,21 +275,33 @@
                 total[half] += factor * moments[s, :, half * LANES : (half + 1) * LANES]
         return total
 
+    packed_groups, pieces = packing(steps, comps)
+
+    def pack(slabs):
+        packed = [jnp.zeros((bricks, LANES), F32) for _ in range(packed_groups)]
+        for k, half, source, group, goal, count in pieces:
+            if slabs[k] is None:
+                continue
+            block = slabs[k][half]
+            if goal != source:
+                block = pltpu.roll(block, (goal - source) % LANES, 1)
+            keep = (lane >= goal) & (lane < goal + count)
+            packed[group] = jnp.where(keep, block, packed[group])
+        return packed
+
     odd = place % 2 == 1
-    empty = [jnp.zeros((bricks, LANES), F32) for _ in range(2)]
-    above = [coefficient(steps + k) if k < 2 else empty for k in range(steps)]
-    below = [coefficient(-1) if k == steps - 1 else empty for k in range(steps)]
-    for k in range(steps):
-        mine = coefficient(k)
-        mine[1] = jnp.where(lane == DEST_AT - LANES, destination, mine[1])
-        for half in range(2):
-            cols = slice(half * LANES, (half + 1) * LANES)
-            own_ref[k, :, cols] = mine[half]
-            send_a_ref[k, :, cols] = jnp.where(odd, below[k][half], above[k][half])
-            send_b_ref[k, :, cols] = jnp.where(odd, above[k][half], below[k][half])
-
-
-def split3(x):
+    above = pack([coefficient(steps + k) if k < 2 else None for k in range(steps)])
+    below = pack([coefficient(-1) if k == steps - 1 else None for k in range(steps)])
+    mine = pack([coefficient(k) for k in range(steps)])
+    mine[-1] = jnp.where(lane == LANES - 1, destination, mine[-1])
+    for group in range(packed_groups):
+        cols = slice(group * LANES, (group + 1) * LANES)
+        send_b_ref[:, cols] = jnp.where(odd, above[group], below[group])
+        send_a_ref[:, cols] = jnp.where(odd, below[group], above[group])
+        own_ref[:, cols] = mine[group]
+
+
+def split(x):
     high = x.astype(BF16)
     rest = x - high.astype(F32)
     middle = rest.astype(BF16)
@@ -253,33 +311,34 @@
 def expand_kernel(capacity, count, *refs):
     blocks = refs[:count]
     hessian_table, gradient_table, hessian_ref, gradient_ref = refs[count:]
-    steps, bricks, _ = blocks[0].shape
-    slots = hessian_ref.shape[1]
+    bricks, width = blocks[0].shape
+    steps, slots, _ = hessian_ref.shape
+    dofs = gradient_ref.shape[1]
     me = lax.axis_index("space")
     slot = lax.broadcasted_iota(jnp.int32, (bricks, slots), 1).astype(F32)
     picks = []
     for distance, block in enumerate(blocks):
         source = (me + count - distance) % count
-        rank = block[0, :, DEST_AT : DEST_AT + 1] - (me * capacity).astype(F32)
+        rank = block[:, width - 1 :] - (me * capacity).astype(F32)
         mine = (rank >= 0.0) & (rank < capacity)
         goal = jnp.where(mine, rank + (source * capacity).astype(F32), -1.0)
         picks.append(jnp.where(slot == goal, 1.0, 0.0))
     pick = jnp.concatenate(picks, axis=0).astype(BF16)
+    values = jnp.concatenate([block[...] for block in blocks], axis=0)
+    placed = [
+        lax.dot_general(pick, part, (((0,), (0,)), ((), ())), preferred_element_type=F32).astype(BF16)
+        for part in split(values)
+    ]
     for k in range(steps):
-        values = jnp.concatenate([block[k] for block in blocks], axis=0)
-        hessian = gradient = None
-        for part in split3(values):
-            placed = lax.dot_general(
-                pick, part, (((0,), (0,)), ((), ())), preferred_element_type=F32
-            ).astype(BF16)
-            wide = jnp.dot(placed, hessian_table[...], preferred_element_type=F32)
-            thin = lax.dot_general(
-                gradient_table[...], placed, (((1,), (1,)), ((), ())), preferred_element_type=F32
-            )
-            hessian = wide if hessian is None else hessian + wide
-            gradient = thin if gradient is None else gradient + thin
-        hessian_ref[k] = hessian
-        gradient_ref[k] = gradient
+        hessian_ref[k] = sum(
+            jnp.dot(part, hessian_table[k], preferred_element_type=F32) for part in placed
+        )
+    gradient = sum(
+        lax.dot_general(gradient_table[...], part, (((1,), (1,)), ((), ())), preferred_element_type=F32)
+        for part in placed
+    )
+    for k in range(steps):
+        gradient_ref[k] = gradient[k * dofs : (k + 1) * dofs]
 
 
 def per_device(image_gradient, residual, phase, counts, owner):
@@ -289,13 +348,13 @@
     capacity = 3 * bricks // (2 * spaces)
     dofs = NODES * comps
     groups = len(component_pairs(comps)) + comps
-    parts = 2
-    width = voxels // parts
+    parts = voxel_parts(voxels, (4, 4, 4, 4))
+    widest = max(width for _, width in parts)
     table, scale = voxel_tables(voxels)
-    block = (steps, bricks, WIDTH)
+    block = (bricks, packing(steps, comps)[0] * LANES)
     in_hbm = pl.BlockSpec(memory_space=pltpu.HBM)
     own, send_a, send_b = pl.pallas_call(
-        functools.partial(moments_kernel, capacity),
+        functools.partial(moments_kernel, capacity, parts, 2),
         in_specs=[in_hbm] * 7,
         out_shape=[pltpu.VMEM(block, F32)] * 3,
         scratch_shapes=[
@@ -306,13 +365,13 @@
             pltpu.VMEM((1, steps), F32),
             pltpu.VMEM((voxels, LANES), BF16),
             pltpu.VMEM(scale.shape, BF16),
-            pltpu.VMEM((groups * steps * bricks, width), BF16),
-            pltpu.VMEM((groups * steps * bricks, width), BF16),
+            pltpu.VMEM((groups * steps * bricks, widest), BF16),
+            pltpu.VMEM((groups * steps * bricks, widest), BF16),
             pltpu.VMEM((bricks, round(voxels ** (2 / 3))), jnp.int32),
             pltpu.VMEM((groups * steps * bricks, LANES), F32),
-            pltpu.VMEM(block, F32),
+            pltpu.VMEM((steps, bricks, 2 * LANES), F32),
             pltpu.SemaphoreType.DMA((4,)),
-            pltpu.SemaphoreType.DMA((parts, 3)),
+            pltpu.SemaphoreType.DMA((len(parts), 3)),
         ],
         compiler_params=pltpu.CompilerParams(vmem_limit_bytes=32 << 20),
         name="moments",
@@ -341,7 +400,7 @@
     for distance in range(1, spaces):
         route = [(i, (i + distance) % spaces) for i in range(spaces)]
         blocks.append(lax.ppermute(total, "space", route))
-    hessian_table, gradient_table = expansion_tables(comps)
+    hessian_table, gradient_table = expansion_tables(steps, comps)
     hessian, gradient = pl.pallas_call(
         functools.partial(expand_kernel, capacity, spaces),
         out_shape=[

time: 20.6 us -> 19.4 us (0.942)
  Pallas kernels: 7.77 us -> 7.04 us
  waiting for transfers between devices: 5.48 us -> 5.08 us
    pallas_call x1, Pallas kernels: 5.87 us -> 5.27 us  [per_device(): pl.pallas_call(functools.partial(moments_kernel, capacity, parts, 2), in_...]
    ppermute x2, waiting for transfers between devices: 4.5 us -> 4.14 us  [exchange(): lax.ppermute(values, 'tm', route)]
  transfers between devices with their start and end apart: 3 -> 3, of which waited for: 3 -> 2; matrix products, arithmetic and copies ran while one was open for 0% -> 0% of each run, Pallas kernels for 0% -> 0%
where the time goes in v3:
time: 19.4 us; the launch traced here: 19.3 us
  Pallas kernels  7.04 us (36%)
  starting transfers between devices  6.44 us (33%)
  waiting for transfers between devices  5.08 us (26%)
  between operations  0.68 us (4%)
    pallas_call x1, Pallas kernels, per_device(): pl.pallas_call(functools.partial(moments_kernel, capacity, parts, 2), in_...  5.27 us
    ppermute x2, starting transfers between devices, exchange(): lax.ppermute(values, 'tm', route)  4.27 us
    ppermute x2, waiting for transfers between devices, exchange(): lax.ppermute(values, 'tm', route)  4.14 us
    ppermute x1, starting transfers between devices, per_device(): blocks.append(lax.ppermute(total, 'space', route))  2.17 us
    pallas_call x1, Pallas kernels, per_device(): pl.pallas_call(functools.partial(expand_kernel, capacity, spaces), out_sh...  1.78 us
    ppermute x1, waiting for transfers between devices, per_device(): blocks.append(lax.ppermute(total, 'space', route))  0.94 us
  transfers between devices with their start and end apart: 3, of which 2 were waited for; matrix products, arithmetic and copies ran while one was open for 0% of the time, Pallas kernels for 0%

profile of v3, /device:TPU:17, one launch (start us, length us, event | category | flops | bytes accessed | tf_op | source)
XLA Modules:
  0.0 19.3 jit_solution(6687411391483119399)
XLA Ops:
  0.6 0.0 copy-start.1
  0.6 0.0 copy-start
  0.7 5.3 %moments.1 = (f32[64,384]{1,0:T(8,128)S(1)}, f32[64,384]{1,0:T(8,128)S(1)}, f32[64,384]{1,0:T(8,128)S(1)}) custom-call(bf16[2,3,64,4096]{3,2,1,0:T(8,128)(2,1)} %bitcast.5, bf16[2,64,4096]{2,1,0:T(8,128)(2,1)} %resid_hbm.1, s32[1,64]{1,0:T(1,128)} %bitcast.6, s32[1,64]{1,0:T(1,128)} %bitcast.7, f32[1,2]{1,0:T(1,128)} %bitcast.8, ...), custom_call_target="tpu_custom_call" | custom-call | tf_op jit(solution)/shard_map/moments/pallas_call | solution.py:356
  5.9 1.3 %collective-permute-start = (f32[64,384]{1,0:T(8,128)S(1)}, f32[64,384]{1,0:T(8,128)S(1)}, u32[]{:S(2)}, u32[]{:S(2)}) collective-permute-start(f32[64,384]{1,0:T(8,128)S(1)} %get-tuple-element.8), channel_id=1, source_target_pairs={{0,2},{4,6},{8,10},{12,14},{16,18},{20,22},{24,26},{28,30},{2,0},{... | collective-permute-start | bytes 294920 | tf_op jit(solution)/shard_map/ppermute | solution.py:396
  7.2 3.0 %collective-permute-start.1 = (f32[64,384]{1,0:T(8,128)S(1)}, f32[64,384]{1,0:T(8,128)S(1)}, u32[]{:S(2)}, u32[]{:S(2)}) collective-permute-start(f32[64,384]{1,0:T(8,128)S(1)} %get-tuple-element.9), channel_id=1, source_target_pairs={{2,4},{6,8},{10,12},{14,16},{18,20},{22,24},{26,28},{4,2},{8,6},{1... | collective-permute-start | bytes 294920 | tf_op jit(solution)/shard_map/ppermute | solution.py:396
  10.2 0.0 collective-permute-done
  10.2 4.1 %collective-permute-done.1 = f32[64,384]{1,0:T(8,128)S(1)} collective-permute-done((f32[64,384]{1,0:T(8,128)S(1)}, f32[64,384]{1,0:T(8,128)S(1)}, u32[]{:S(2)}, u32[]{:S(2)}) %collective-permute-start.1) | collective-permute-done | bytes 98336 | tf_op jit(solution)/shard_map/ppermute | solution.py:396
  14.4 2.2 %collective-permute-start.2 = (f32[64,384]{1,0:T(8,128)S(1)}, f32[64,384]{1,0:T(8,128)S(1)}, u32[]{:S(2)}, u32[]{:S(2)}) collective-permute-start(f32[64,384]{1,0:T(8,128)S(1)} %add_add_fusion.refs_0_), channel_id=1, source_target_pairs={{0,1},{1,0},{2,3},{3,2},{4,5},{5,4},{6,7},{7,6},{8,9},{9,8},{10,11... | collective-permute-start | bytes 294920 | tf_op jit(solution)/shard_map/ppermute | solution.py:402
  16.6 0.9 %collective-permute-done.2.refs_1_ = f32[64,384]{1,0:T(8,128)S(1)} collective-permute-done((f32[64,384]{1,0:T(8,128)S(1)}, f32[64,384]{1,0:T(8,128)S(1)}, u32[]{:S(2)}, u32[]{:S(2)}) %collective-permute-start.2) | collective-permute-done | bytes 98336 | tf_op jit(solution)/shard_map/ppermute | solution.py:402
  17.5 0.0 copy-done.1
  17.5 0.0 copy-done
  17.5 1.8 %expand.1 = (f32[2,96,576]{2,1,0:T(8,128)}, f32[2,24,96]{2,1,0:T(8,128)}) custom-call(f32[64,384]{1,0:T(8,128)S(1)} %add_add_fusion.refs_0_, f32[64,384]{1,0:T(8,128)S(1)} %collective-permute-done.2.refs_1_, bf16[2,384,576]{2,1,0:T(8,128)(2,1)S(1)} %copy-done, bf16[48,384]{1,0:T(8,128)(2,1)S(1)} %copy-done.1), custom_call_target="tpu_custom_call" | custom-call | tf_op jit(solution)/shard_map/expand/pallas_call | solution.py:404
  (1 shorter events, 0.0 us)
Async XLA Ops:
  0.6 16.9 %copy-start.1 = (bf16[48,384]{1,0:T(8,128)(2,1)S(1)}, bf16[48,384]{1,0:T(8,128)(2,1)}, u32[]{:S(2)}) copy-start(bf16[48,384]{1,0:T(8,128)(2,1)} %constant.11.clone.refs_3_) | copy-start | bytes 110596
  0.6 16.9 %copy-start = (bf16[2,384,576]{2,1,0:T(8,128)(2,1)S(1)}, bf16[2,384,576]{2,1,0:T(8,128)(2,1)}, u32[]{:S(2)}) copy-start(bf16[2,384,576]{2,1,0:T(8,128)(2,1)} %constant.10.clone.refs_2_) | copy-start | bytes 2654212
  5.9 4.3 %collective-permute-start = (f32[64,384]{1,0:T(8,128)S(1)}, f32[64,384]{1,0:T(8,128)S(1)}, u32[]{:S(2)}, u32[]{:S(2)}) collective-permute-start(f32[64,384]{1,0:T(8,128)S(1)} %get-tuple-element.8), channel_id=1, source_target_pairs={{0,2},{4,6},{8,10},{12,14},{16,18},{20,22},{24,26},{28,30},{2,0},{... | collective-permute-start | bytes 294920 | tf_op jit(solution)/shard_map/ppermute | solution.py:396
  7.2 7.1 %collective-permute-start.1 = (f32[64,384]{1,0:T(8,128)S(1)}, f32[64,384]{1,0:T(8,128)S(1)}, u32[]{:S(2)}, u32[]{:S(2)}) collective-permute-start(f32[64,384]{1,0:T(8,128)S(1)} %get-tuple-element.9), channel_id=1, source_target_pairs={{2,4},{6,8},{10,12},{14,16},{18,20},{22,24},{26,28},{4,2},{8,6},{1... | collective-permute-start | bytes 294920 | tf_op jit(solution)/shard_map/ppermute | solution.py:396
  14.4 3.1 %collective-permute-start.2 = (f32[64,384]{1,0:T(8,128)S(1)}, f32[64,384]{1,0:T(8,128)S(1)}, u32[]{:S(2)}, u32[]{:S(2)}) collective-permute-start(f32[64,384]{1,0:T(8,128)S(1)} %add_add_fusion.refs_0_), channel_id=1, source_target_pairs={{0,1},{1,0},{2,3},{3,2},{4,5},{5,4},{6,7},{7,6},{8,9},{9,8},{10,11... | collective-permute-start | bytes 294920 | tf_op jit(solution)/shard_map/ppermute | solution.py:402

commit v4 on v3

--- a/solution.py
+++ b/solution.py
@@ -129,22 +129,26 @@
     scale_hbm,
     own_ref,
     send_a_ref,
-    send_b_ref,
-    grads,
-    resid,
-    counts_ref,
-    owner_ref,
-    phase_ref,
-    table,
-    scale,
-    products_a,
-    products_b,
-    limits,
-    sums,
-    moments,
-    small_sems,
-    sems,
+    *refs,
 ):
+    spaces = lax.axis_size("space")
+    send_b_refs, refs = refs[:spaces], refs[spaces:]
+    (
+        grads,
+        resid,
+        counts_ref,
+        owner_ref,
+        phase_ref,
+        table,
+        scale,
+        products_a,
+        products_b,
+        limits,
+        sums,
+        moments,
+        small_sems,
+        sems,
+    ) = refs
     steps, comps, bricks, voxels = grads.shape
     pairs = component_pairs(comps)
     groups = len(pairs) + comps
@@ -225,6 +229,15 @@
     same = (owner_col == owner_row) & earlier
     rank = jnp.sum(jnp.where(same, 1.0, 0.0), axis=1, keepdims=True)
     destination = owner_col * capacity + rank
+    later = lax.broadcasted_iota(jnp.int32, square, 1) > lax.broadcasted_iota(jnp.int32, square, 0)
+    before = jnp.where((owner_col == owner_row) & later, 1.0, 0.0)
+    destination_row = owner_row * capacity + jnp.sum(before, axis=0, keepdims=True)
+    me = lax.axis_index("space")
+    slot = lax.broadcasted_iota(jnp.int32, (capacity, bricks), 0)
+    picks = []
+    for distance in range(spaces):
+        goal = (slot + (me + distance) % spaces * capacity).astype(F32)
+        picks.append(jnp.where(goal == destination_row, 1.0, 0.0).astype(BF16))
 
     for k in range(len(parts)):
         for copy in copies(k):
@@ -292,53 +305,65 @@
     odd = place % 2 == 1
     above = pack([coefficient(steps + k) if k < 2 else None for k in range(steps)])
     below = pack([coefficient(-1) if k == steps - 1 else None for k in range(steps)])
+    for group in range(packed_groups):
+        cols = slice(group * LANES, (group + 1) * LANES)
+        parts_b = split(jnp.where(odd, above[group], below[group]))
+        for pick, ref in zip(picks, send_b_refs):
+            ref[:, cols] = sum(jnp.dot(pick, part, preferred_element_type=F32) for part in parts_b)
+        send_a_ref[:, cols] = jnp.where(odd, below[group], above[group])
     mine = pack([coefficient(k) for k in range(steps)])
     mine[-1] = jnp.where(lane == LANES - 1, destination, mine[-1])
     for group in range(packed_groups):
-        cols = slice(group * LANES, (group + 1) * LANES)
-        send_b_ref[:, cols] = jnp.where(odd, above[group], below[group])
-        send_a_ref[:, cols] = jnp.where(odd, below[group], above[group])
-        own_ref[:, cols] = mine[group]
+        own_ref[:, group * LANES : (group + 1) * LANES] = mine[group]
 
 
 def split(x):
     high = x.astype(BF16)
-    rest = x - high.astype(F32)
-    middle = rest.astype(BF16)
-    return high, middle, (rest - middle.astype(F32)).astype(BF16)
-
-
-def expand_kernel(capacity, count, *refs):
-    blocks = refs[:count]
-    hessian_table, gradient_table, hessian_ref, gradient_ref = refs[count:]
-    bricks, width = blocks[0].shape
-    steps, slots, _ = hessian_ref.shape
-    dofs = gradient_ref.shape[1]
+    return high, (x - high.astype(F32)).astype(BF16)
+
+
+def place_kernel(capacity, *refs):
+    *blocks, out_ref = refs
     me = lax.axis_index("space")
-    slot = lax.broadcasted_iota(jnp.int32, (bricks, slots), 1).astype(F32)
-    picks = []
+    width = out_ref.shape[1]
     for distance, block in enumerate(blocks):
-        source = (me + count - distance) % count
-        rank = block[:, width - 1 :] - (me * capacity).astype(F32)
-        mine = (rank >= 0.0) & (rank < capacity)
-        goal = jnp.where(mine, rank + (source * capacity).astype(F32), -1.0)
-        picks.append(jnp.where(slot == goal, 1.0, 0.0))
-    pick = jnp.concatenate(picks, axis=0).astype(BF16)
-    values = jnp.concatenate([block[...] for block in blocks], axis=0)
-    placed = [
-        lax.dot_general(pick, part, (((0,), (0,)), ((), ())), preferred_element_type=F32).astype(BF16)
-        for part in split(values)
-    ]
+        slot = lax.broadcasted_iota(jnp.int32, (block.shape[0], capacity), 1)
+        goal = (slot + me * capacity).astype(F32)
+        pick = jnp.where(goal == block[:, width - 1 :], 1.0, 0.0).astype(BF16)
+        out_ref[distance * capacity : (distance + 1) * capacity] = sum(
+            lax.dot_general(pick, part, (((0,), (0,)), ((), ())), preferred_element_type=F32)
+            for part in split(block[...])
+        )
+
+
+def expand_kernel(
+    capacity, ready, last, table, gradient_table, hessian_hbm, gradient_hbm, total, wide, thin, sems
+):
+    steps, slots, _ = wide.shape
+    dofs = thin.shape[1]
+    spaces = slots // capacity
+    me = lax.axis_index("space")
+    for distance in range(spaces):
+        here = slice(distance * capacity, (distance + 1) * capacity)
+        source = (me + spaces - distance) % spaces
+        rows = pl.ds(pl.multiple_of(source * capacity, math.gcd(capacity, 8)), capacity)
+        total[rows] = ready[here] + last[here]
+    parts = split(total[...])
+    copies = []
     for k in range(steps):
-        hessian_ref[k] = sum(
-            jnp.dot(part, hessian_table[k], preferred_element_type=F32) for part in placed
-        )
+        wide[k] = sum(jnp.dot(part, table[k], preferred_element_type=F32) for part in parts)
+        copies.append(pltpu.make_async_copy(wide.at[k], hessian_hbm.at[k], sems.at[k]))
+        copies[-1].start()
     gradient = sum(
         lax.dot_general(gradient_table[...], part, (((1,), (1,)), ((), ())), preferred_element_type=F32)
-        for part in placed
+        for part in parts
     )
     for k in range(steps):
-        gradient_ref[k] = gradient[k * dofs : (k + 1) * dofs]
+        thin[k] = gradient[k * dofs : (k + 1) * dofs]
+    copies.append(pltpu.make_async_copy(thin, gradient_hbm, sems.at[steps]))
+    copies[-1].start()
+    for copy in copies:
+        copy.wait()
 
 
 def per_device(image_gradient, residual, phase, counts, owner):
@@ -353,10 +378,10 @@
     table, scale = voxel_tables(voxels)
     block = (bricks, packing(steps, comps)[0] * LANES)
     in_hbm = pl.BlockSpec(memory_space=pltpu.HBM)
-    own, send_a, send_b = pl.pallas_call(
+    own, send_a, *send_b = pl.pallas_call(
         functools.partial(moments_kernel, capacity, parts, 2),
         in_specs=[in_hbm] * 7,
-        out_shape=[pltpu.VMEM(block, F32)] * 3,
+        out_shape=[pltpu.VMEM(block, F32)] * 2 + [pltpu.VMEM((capacity, block[1]), F32)] * spaces,
         scratch_shapes=[
             pltpu.VMEM((steps, comps, bricks, voxels), BF16),
             pltpu.VMEM((steps, bricks, voxels), BF16),
@@ -395,21 +420,37 @@
         route = [(i, i + 1) for i in lower] + [(i + 1, i) for i in lower]
         return lax.ppermute(values, "tm", route) if route else jnp.zeros_like(values)
 
-    total = own + exchange(send_a, 0) + exchange(send_b, 1)
-    blocks = [total]
-    for distance in range(1, spaces):
+    def turned(values, distance):
         route = [(i, (i + distance) % spaces) for i in range(spaces)]
-        blocks.append(lax.ppermute(total, "space", route))
-    hessian_table, gradient_table = expansion_tables(steps, comps)
+        return lax.ppermute(values, "space", route) if distance else values
+
+    for_far = jnp.concatenate([turned(x, distance) for distance, x in enumerate(send_b)])
+    near = own + exchange(send_a, 0)
+    last = exchange(for_far, 1)
+    blocks = [turned(near, distance) for distance in range(spaces)]
+    slots = spaces * capacity
+    ready = pl.pallas_call(
+        functools.partial(place_kernel, capacity),
+        out_shape=pltpu.VMEM((slots, block[1]), F32),
+        compiler_params=pltpu.CompilerParams(vmem_limit_bytes=8 << 20),
+        name="place",
+    )(*blocks)
+    hessian_table, gradient_table = (jnp.asarray(x) for x in expansion_tables(steps, comps))
+    wide = (steps, slots, dofs * dofs)
+    thin = (steps, dofs, slots)
     hessian, gradient = pl.pallas_call(
-        functools.partial(expand_kernel, capacity, spaces),
-        out_shape=[
-            jax.ShapeDtypeStruct((steps, spaces * capacity, dofs * dofs), F32),
-            jax.ShapeDtypeStruct((steps, dofs, spaces * capacity), F32),
+        functools.partial(expand_kernel, capacity),
+        out_shape=[jax.ShapeDtypeStruct(wide, F32), jax.ShapeDtypeStruct(thin, F32)],
+        out_specs=[in_hbm] * 2,
+        scratch_shapes=[
+            pltpu.VMEM((slots, block[1]), F32),
+            pltpu.VMEM(wide, F32),
+            pltpu.VMEM(thin, F32),
+            pltpu.SemaphoreType.DMA((steps + 1,)),
         ],
         compiler_params=pltpu.CompilerParams(vmem_limit_bytes=16 << 20),
         name="expand",
-    )(*blocks, jnp.asarray(hessian_table), jnp.asarray(gradient_table))
+    )(ready, last, hessian_table, gradient_table)
     return hessian, jnp.transpose(gradient, (0, 2, 1))
 
 

time: 19.4 us -> 18.8 us (0.969)
  the two profiles are of different devices: /device:TPU:17 before, /device:TPU:24 now
where the time goes in v4:
time: 18.8 us; the launch traced here: 18.6 us
  Pallas kernels  6.98 us (37%)
  starting transfers between devices  5.63 us (30%)
  waiting for transfers between devices  5.28 us (28%)
  between operations  0.7 us (4%)
    ppermute x2, starting transfers between devices, exchange(): lax.ppermute(values, 'tm', route)  5.49 us
    pallas_call x1, Pallas kernels, per_device(): pl.pallas_call(functools.partial(moments_kernel, capacity, parts, 2), in_...  5.42 us
    ppermute x2, waiting for transfers between devices, exchange(): lax.ppermute(values, 'tm', route)  3.99 us
    ppermute x2, waiting for transfers between devices, turned(): return lax.ppermute(values, 'space', route) if distance else values  1.29 us
    pallas_call x1, Pallas kernels, per_device(): pl.pallas_call(functools.partial(expand_kernel, capacity), out_shape=[jax...  1.28 us
  transfers between devices with their start and end apart: 4, of which 2 were waited for; matrix products, arithmetic and copies ran while one was open for 0% of the time, Pallas kernels for 2%

profile of v4, /device:TPU:24, one launch (start us, length us, event | category | flops | bytes accessed | tf_op | source)
XLA Modules:
  0.0 18.6 jit_solution(7563837798915327345)
XLA Ops:
  0.6 0.0 copy-start
  0.6 0.0 copy-start.1
  0.7 5.4 %moments.1 = (f32[64,384]{1,0:T(8,128)S(1)}, f32[64,384]{1,0:T(8,128)S(1)}, f32[48,384]{1,0:T(8,128)S(1)}, f32[48,384]{1,0:T(8,128)S(1)}) custom-call(bf16[2,3,64,4096]{3,2,1,0:T(8,128)(2,1)} %bitcast.5, bf16[2,64,4096]{2,1,0:T(8,128)(2,1)} %resid_hbm.1, s32[1,64]{1,0:T(1,128)} %bitcast.6, s32[1,64]{1,0:T(1,128)} %bitcast.7, f32[1,2]{1,0:T(1,128)} %bitcast.8, ...), custom_call_target="tpu_custom_call" | custom-call | tf_op jit(solution)/shard_map/moments/pallas_call | solution.py:381
  6.1 0.1 collective-permute-start.2
  6.2 1.6 %collective-permute-start = (f32[64,384]{1,0:T(8,128)S(1)}, f32[64,384]{1,0:T(8,128)S(1)}, u32[]{:S(2)}, u32[]{:S(2)}) collective-permute-start(f32[64,384]{1,0:T(8,128)S(1)} %get-tuple-element.9), channel_id=1, source_target_pairs={{0,2},{4,6},{8,10},{12,14},{16,18},{20,22},{24,26},{28,30},{2,0},{... | collective-permute-start | bytes 294920 | tf_op jit(solution)/shard_map/ppermute | solution.py:421
  7.7 0.0 collective-permute-done.2
  7.7 3.9 %collective-permute-start.3 = (f32[96,384]{1,0:T(8,128)S(1)}, f32[96,384]{1,0:T(8,128)S(1)}, u32[]{:S(2)}, u32[]{:S(2)}) collective-permute-start(f32[96,384]{1,0:T(8,128)S(1)} %pad_maximum_fusion), channel_id=1, source_target_pairs={{2,4},{6,8},{10,12},{14,16},{18,20},{22,24},{26,28},{4,2},{8,6},{1... | collective-permute-start | bytes 442376 | tf_op jit(solution)/shard_map/ppermute | solution.py:421
  11.7 0.0 collective-permute-done
  11.7 0.1 collective-permute-start.1
  11.8 1.3 %collective-permute-done.1.refs_1_ = f32[64,384]{1,0:T(8,128)S(1)} collective-permute-done((f32[64,384]{1,0:T(8,128)S(1)}, f32[64,384]{1,0:T(8,128)S(1)}, u32[]{:S(2)}, u32[]{:S(2)}) %collective-permute-start.1) | collective-permute-done | bytes 98336 | tf_op jit(solution)/shard_map/ppermute | solution.py:425
  13.1 0.3 %place.1.ready = f32[96,384]{1,0:T(8,128)S(1)} custom-call(f32[64,384]{1,0:T(8,128)S(1)} %add.3.refs_0_, f32[64,384]{1,0:T(8,128)S(1)} %collective-permute-done.1.refs_1_), custom_call_target="tpu_custom_call" | custom-call | tf_op jit(solution)/shard_map/place/pallas_call | solution.py:432
  13.4 4.0 %collective-permute-done.3.last = f32[96,384]{1,0:T(8,128)S(1)} collective-permute-done((f32[96,384]{1,0:T(8,128)S(1)}, f32[96,384]{1,0:T(8,128)S(1)}, u32[]{:S(2)}, u32[]{:S(2)}) %collective-permute-start.3) | collective-permute-done | bytes 147488 | tf_op jit(solution)/shard_map/ppermute | solution.py:421
  17.3 0.0 copy-done
  17.3 0.0 copy-done.1
  17.3 1.3 %expand.1 = (f32[2,96,576]{2,1,0:T(8,128)}, f32[2,24,96]{2,1,0:T(8,128)}) custom-call(f32[96,384]{1,0:T(8,128)S(1)} %place.1.ready, f32[96,384]{1,0:T(8,128)S(1)} %collective-permute-done.3.last, bf16[2,384,576]{2,1,0:T(8,128)(2,1)S(1)} %copy-done, bf16[48,384]{1,0:T(8,128)(2,1)S(1)} %copy-done.1), custom_call_target="tpu_custom_call" | custom-call | tf_op jit(solution)/shard_map/expand/pallas_call | solution.py:441
  (2 shorter events, 0.0 us)
Async XLA Ops:
  0.6 16.7 %copy-start = (bf16[2,384,576]{2,1,0:T(8,128)(2,1)S(1)}, bf16[2,384,576]{2,1,0:T(8,128)(2,1)}, u32[]{:S(2)}) copy-start(bf16[2,384,576]{2,1,0:T(8,128)(2,1)} %constant.10.clone.table) | copy-start | bytes 2654212
  0.6 16.7 %copy-start.1 = (bf16[48,384]{1,0:T(8,128)(2,1)S(1)}, bf16[48,384]{1,0:T(8,128)(2,1)}, u32[]{:S(2)}) copy-start(bf16[48,384]{1,0:T(8,128)(2,1)} %constant.11.clone.gradient_table) | copy-start | bytes 110596
  6.1 1.6 %collective-permute-start.2 = (f32[48,384]{1,0:T(8,128)S(1)}, f32[48,384]{1,0:T(8,128)S(1)}, u32[]{:S(2)}, u32[]{:S(2)}) collective-permute-start(f32[48,384]{1,0:T(8,128)S(1)} %get-tuple-element.11), channel_id=1, source_target_pairs={{0,1},{1,0},{2,3},{3,2},{4,5},{5,4},{6,7},{7,6},{8,9},{9,8},{10,11... | collective-permute-start | bytes 221192 | tf_op jit(solution)/shard_map/ppermute | solution.py:425
  6.2 5.5 %collective-permute-start = (f32[64,384]{1,0:T(8,128)S(1)}, f32[64,384]{1,0:T(8,128)S(1)}, u32[]{:S(2)}, u32[]{:S(2)}) collective-permute-start(f32[64,384]{1,0:T(8,128)S(1)} %get-tuple-element.9), channel_id=1, source_target_pairs={{0,2},{4,6},{8,10},{12,14},{16,18},{20,22},{24,26},{28,30},{2,0},{... | collective-permute-start | bytes 294920 | tf_op jit(solution)/shard_map/ppermute | solution.py:421
  7.7 9.6 %collective-permute-start.3 = (f32[96,384]{1,0:T(8,128)S(1)}, f32[96,384]{1,0:T(8,128)S(1)}, u32[]{:S(2)}, u32[]{:S(2)}) collective-permute-start(f32[96,384]{1,0:T(8,128)S(1)} %pad_maximum_fusion), channel_id=1, source_target_pairs={{2,4},{6,8},{10,12},{14,16},{18,20},{22,24},{26,28},{4,2},{8,6},{1... | collective-permute-start | bytes 442376 | tf_op jit(solution)/shard_map/ppermute | solution.py:421
  11.7 1.4 %collective-permute-start.1 = (f32[64,384]{1,0:T(8,128)S(1)}, f32[64,384]{1,0:T(8,128)S(1)}, u32[]{:S(2)}, u32[]{:S(2)}) collective-permute-start(f32[64,384]{1,0:T(8,128)S(1)} %add.3.refs_0_), channel_id=1, source_target_pairs={{0,1},{1,0},{2,3},{3,2},{4,5},{5,4},{6,7},{7,6},{8,9},{9,8},{10,11... | collective-permute-start | bytes 294920 | tf_op jit(solution)/shard_map/ppermute | solution.py:425

commit v5 on v4

--- a/solution.py
+++ b/solution.py
@@ -119,7 +119,6 @@
 def moments_kernel(
     capacity,
     parts,
-    ahead,
     grads_hbm,
     resid_hbm,
     counts_hbm,
@@ -178,9 +177,9 @@
 
     for copy in small:
         copy.start()
-    for k in range(ahead):
+    for k in range(len(parts)):
         for copy in copies(k):
-            copy.start()
+            copy.start(priority=min(k, 1))
 
     lane = lax.broadcasted_iota(jnp.int32, (1, LANES), 1)
     tall = math.gcd(bricks, 16)
@@ -239,12 +238,38 @@
         goal = (slot + (me + distance) % spaces * capacity).astype(F32)
         picks.append(jnp.where(goal == destination_row, 1.0, 0.0).astype(BF16))
 
+    place = lax.axis_index("tm")
+    places = lax.axis_size("tm")
+    first_step = place * steps
+    odd = place % 2 == 1
+    weights = [spline_weights(phase_ref[:, s : s + 1]) for s in range(steps)]
+    factors = {}
+    for s in range(steps):
+        for position in range(-1, steps + 2):
+            basis = None
+            for j in range(4):
+                reach = s - 1 + j
+                if position not in (reach, max(reach, 0), min(reach, steps - 1)):
+                    continue
+                goal = jnp.clip(first_step + reach, 0, places * steps - 1) - first_step
+                term = jnp.where(goal == position, weights[s][j], 0.0)
+                basis = term if basis is None else basis + term
+            if basis is not None:
+                factors[position, s] = jnp.where(lane < GRAD_AT, basis * basis, basis)
+
+    def coefficient(position):
+        return [
+            sum(
+                factors[position, s] * moments[s, :, half * LANES : (half + 1) * LANES]
+                for s in range(steps)
+                if (position, s) in factors
+            )
+            for half in range(2)
+        ]
+
     for k in range(len(parts)):
         for copy in copies(k):
             copy.wait()
-        if k + ahead < len(parts):
-            for copy in copies(k + ahead):
-                copy.start()
         fill(k, buffers[k % 2])
         reduce(k, buffers[k % 2])
 
@@ -267,27 +292,6 @@
             whole = halves[half] + jnp.where(lane >= GRAD_AT, low, 0.0)
             moments[s, :, half * LANES : (half + 1) * LANES] = whole
 
-    place = lax.axis_index("tm")
-    places = lax.axis_size("tm")
-    first_step = place * steps
-    weights = [spline_weights(phase_ref[:, s : s + 1]) for s in range(steps)]
-
-    def coefficient(position):
-        total = [jnp.zeros((bricks, LANES), F32) for _ in range(2)]
-        for s in range(steps):
-            basis = jnp.zeros((1, 1), F32)
-            for j in range(4):
-                reach = s - 1 + j
-                if position not in (reach, max(reach, 0), min(reach, steps - 1)):
-                    continue
-                goal = jnp.clip(first_step + reach, 0, places * steps - 1) - first_step
-                basis = basis + jnp.where(goal == position, weights[s][j], 0.0)
-            squared = basis * basis
-            factor = jnp.where(lane < GRAD_AT, squared, basis)
-            for half in range(2):
-                total[half] += factor * moments[s, :, half * LANES : (half + 1) * LANES]
-        return total
-
     packed_groups, pieces = packing(steps, comps)
 
     def pack(slabs):
@@ -302,7 +306,6 @@
             packed[group] = jnp.where(keep, block, packed[group])
         return packed
 
-    odd = place % 2 == 1
     above = pack([coefficient(steps + k) if k < 2 else None for k in range(steps)])
     below = pack([coefficient(-1) if k == steps - 1 else None for k in range(steps)])
     for group in range(packed_groups):
@@ -373,13 +376,13 @@
     capacity = 3 * bricks // (2 * spaces)
     dofs = NODES * comps
     groups = len(component_pairs(comps)) + comps
-    parts = voxel_parts(voxels, (4, 4, 4, 4))
+    parts = voxel_parts(voxels, (2, 6, 8))
     widest = max(width for _, width in parts)
     table, scale = voxel_tables(voxels)
     block = (bricks, packing(steps, comps)[0] * LANES)
     in_hbm = pl.BlockSpec(memory_space=pltpu.HBM)
     own, send_a, *send_b = pl.pallas_call(
-        functools.partial(moments_kernel, capacity, parts, 2),
+        functools.partial(moments_kernel, capacity, parts),
         in_specs=[in_hbm] * 7,
         out_shape=[pltpu.VMEM(block, F32)] * 2 + [pltpu.VMEM((capacity, block[1]), F32)] * spaces,
         scratch_shapes=[

time: 18.8 us -> 18.3 us (0.973)
  Pallas kernels: 6.98 us -> 6.43 us
    pallas_call x1, Pallas kernels: 5.42 us -> 4.86 us  [per_device(): pl.pallas_call(functools.partial(moments_kernel, capacity, parts), in_spe...]
where the time goes in v5:
time: 18.3 us; the launch traced here: 18.1 us
  Pallas kernels  6.43 us (35%)
  starting transfers between devices  5.63 us (31%)
  waiting for transfers between devices  5.3 us (29%)
  between operations  0.7 us (4%)
    ppermute x2, starting transfers between devices, exchange(): lax.ppermute(values, 'tm', route)  5.49 us
    pallas_call x1, Pallas kernels, per_device(): pl.pallas_call(functools.partial(moments_kernel, capacity, parts), in_spe...  4.86 us
    ppermute x2, waiting for transfers between devices, exchange(): lax.ppermute(values, 'tm', route)  4.01 us
    ppermute x2, waiting for transfers between devices, turned(): return lax.ppermute(values, 'space', route) if distance else values  1.29 us
    pallas_call x1, Pallas kernels, per_device(): pl.pallas_call(functools.partial(expand_kernel, capacity), out_shape=[jax...  1.29 us
  transfers between devices with their start and end apart: 4, of which 2 were waited for; matrix products, arithmetic and copies ran while one was open for 0% of the time, Pallas kernels for 2%

profile of v5, /device:TPU:24, one launch (start us, length us, event | category | flops | bytes accessed | tf_op | source)
XLA Modules:
  0.0 18.1 jit_solution(735159132157274121)
XLA Ops:
  0.6 0.0 copy-start
  0.6 0.0 copy-start.1
  0.7 4.9 %moments.1 = (f32[64,384]{1,0:T(8,128)S(1)}, f32[64,384]{1,0:T(8,128)S(1)}, f32[48,384]{1,0:T(8,128)S(1)}, f32[48,384]{1,0:T(8,128)S(1)}) custom-call(bf16[2,3,64,4096]{3,2,1,0:T(8,128)(2,1)} %bitcast.5, bf16[2,64,4096]{2,1,0:T(8,128)(2,1)} %resid_hbm.1, s32[1,64]{1,0:T(1,128)} %bitcast.6, s32[1,64]{1,0:T(1,128)} %bitcast.7, f32[1,2]{1,0:T(1,128)} %bitcast.8, ...), custom_call_target="tpu_custom_call" | custom-call | tf_op jit(solution)/shard_map/moments/pallas_call | solution.py:384
  5.5 0.1 collective-permute-start.2
  5.6 1.6 %collective-permute-start = (f32[64,384]{1,0:T(8,128)S(1)}, f32[64,384]{1,0:T(8,128)S(1)}, u32[]{:S(2)}, u32[]{:S(2)}) collective-permute-start(f32[64,384]{1,0:T(8,128)S(1)} %get-tuple-element.9), channel_id=1, source_target_pairs={{0,2},{4,6},{8,10},{12,14},{16,18},{20,22},{24,26},{28,30},{2,0},{... | collective-permute-start | bytes 294920 | tf_op jit(solution)/shard_map/ppermute | solution.py:424
  7.2 0.0 collective-permute-done.2
  7.2 3.9 %collective-permute-start.3 = (f32[96,384]{1,0:T(8,128)S(1)}, f32[96,384]{1,0:T(8,128)S(1)}, u32[]{:S(2)}, u32[]{:S(2)}) collective-permute-start(f32[96,384]{1,0:T(8,128)S(1)} %pad_maximum_fusion), channel_id=1, source_target_pairs={{2,4},{6,8},{10,12},{14,16},{18,20},{22,24},{26,28},{4,2},{8,6},{1... | collective-permute-start | bytes 442376 | tf_op jit(solution)/shard_map/ppermute | solution.py:424
  11.1 0.0 collective-permute-done
  11.2 0.1 collective-permute-start.1
  11.2 1.3 %collective-permute-done.1.refs_1_ = f32[64,384]{1,0:T(8,128)S(1)} collective-permute-done((f32[64,384]{1,0:T(8,128)S(1)}, f32[64,384]{1,0:T(8,128)S(1)}, u32[]{:S(2)}, u32[]{:S(2)}) %collective-permute-start.1) | collective-permute-done | bytes 98336 | tf_op jit(solution)/shard_map/ppermute | solution.py:428
  12.5 0.3 %place.1.ready = f32[96,384]{1,0:T(8,128)S(1)} custom-call(f32[64,384]{1,0:T(8,128)S(1)} %add.3.refs_0_, f32[64,384]{1,0:T(8,128)S(1)} %collective-permute-done.1.refs_1_), custom_call_target="tpu_custom_call" | custom-call | tf_op jit(solution)/shard_map/place/pallas_call | solution.py:435
  12.8 4.0 %collective-permute-done.3.last = f32[96,384]{1,0:T(8,128)S(1)} collective-permute-done((f32[96,384]{1,0:T(8,128)S(1)}, f32[96,384]{1,0:T(8,128)S(1)}, u32[]{:S(2)}, u32[]{:S(2)}) %collective-permute-start.3) | collective-permute-done | bytes 147488 | tf_op jit(solution)/shard_map/ppermute | solution.py:424
  16.8 0.0 copy-done
  16.8 0.0 copy-done.1
  16.8 1.3 %expand.1 = (f32[2,96,576]{2,1,0:T(8,128)}, f32[2,24,96]{2,1,0:T(8,128)}) custom-call(f32[96,384]{1,0:T(8,128)S(1)} %place.1.ready, f32[96,384]{1,0:T(8,128)S(1)} %collective-permute-done.3.last, bf16[2,384,576]{2,1,0:T(8,128)(2,1)S(1)} %copy-done, bf16[48,384]{1,0:T(8,128)(2,1)S(1)} %copy-done.1), custom_call_target="tpu_custom_call" | custom-call | tf_op jit(solution)/shard_map/expand/pallas_call | solution.py:444
  (2 shorter events, 0.0 us)
Async XLA Ops:
  0.6 16.2 %copy-start = (bf16[2,384,576]{2,1,0:T(8,128)(2,1)S(1)}, bf16[2,384,576]{2,1,0:T(8,128)(2,1)}, u32[]{:S(2)}) copy-start(bf16[2,384,576]{2,1,0:T(8,128)(2,1)} %constant.10.clone.table) | copy-start | bytes 2654212
  0.6 16.2 %copy-start.1 = (bf16[48,384]{1,0:T(8,128)(2,1)S(1)}, bf16[48,384]{1,0:T(8,128)(2,1)}, u32[]{:S(2)}) copy-start(bf16[48,384]{1,0:T(8,128)(2,1)} %constant.11.clone.gradient_table) | copy-start | bytes 110596
  5.5 1.7 %collective-permute-start.2 = (f32[48,384]{1,0:T(8,128)S(1)}, f32[48,384]{1,0:T(8,128)S(1)}, u32[]{:S(2)}, u32[]{:S(2)}) collective-permute-start(f32[48,384]{1,0:T(8,128)S(1)} %get-tuple-element.11), channel_id=1, source_target_pairs={{0,1},{1,0},{2,3},{3,2},{4,5},{5,4},{6,7},{7,6},{8,9},{9,8},{10,11... | collective-permute-start | bytes 221192 | tf_op jit(solution)/shard_map/ppermute | solution.py:428
  5.6 5.5 %collective-permute-start = (f32[64,384]{1,0:T(8,128)S(1)}, f32[64,384]{1,0:T(8,128)S(1)}, u32[]{:S(2)}, u32[]{:S(2)}) collective-permute-start(f32[64,384]{1,0:T(8,128)S(1)} %get-tuple-element.9), channel_id=1, source_target_pairs={{0,2},{4,6},{8,10},{12,14},{16,18},{20,22},{24,26},{28,30},{2,0},{... | collective-permute-start | bytes 294920 | tf_op jit(solution)/shard_map/ppermute | solution.py:424
  7.2 9.6 %collective-permute-start.3 = (f32[96,384]{1,0:T(8,128)S(1)}, f32[96,384]{1,0:T(8,128)S(1)}, u32[]{:S(2)}, u32[]{:S(2)}) collective-permute-start(f32[96,384]{1,0:T(8,128)S(1)} %pad_maximum_fusion), channel_id=1, source_target_pairs={{2,4},{6,8},{10,12},{14,16},{18,20},{22,24},{26,28},{4,2},{8,6},{1... | collective-permute-start | bytes 442376 | tf_op jit(solution)/shard_map/ppermute | solution.py:424
  11.2 1.4 %collective-permute-start.1 = (f32[64,384]{1,0:T(8,128)S(1)}, f32[64,384]{1,0:T(8,128)S(1)}, u32[]{:S(2)}, u32[]{:S(2)}) collective-permute-start(f32[64,384]{1,0:T(8,128)S(1)} %add.3.refs_0_), channel_id=1, source_target_pairs={{0,1},{1,0},{2,3},{3,2},{4,5},{5,4},{6,7},{7,6},{8,9},{9,8},{10,11... | collective-permute-start | bytes 294920 | tf_op jit(solution)/shard_map/ppermute | solution.py:428

commit v6 on v5

--- a/solution.py
+++ b/solution.py
@@ -60,44 +60,46 @@
     places = [pair_place(i) for i in range(len(component_pairs(comps)))]
     for half, at, count in places + [gradient_place(c) for c in range(comps)]:
         ends[half] = max(ends[half], at + count)
-    groups = -(-(steps * sum(ends) + 1) // LANES)
-    free = [[g, 0, LANES - (g == groups - 1)] for g in range(groups)]
+    first = LANES - ends[0]
+    rest = ends[1] - first
+    assert 0 < 2 * rest < LANES
     pieces = []
-    for step, half in sorted(np.ndindex(steps, 2), key=lambda x: -ends[x[1]]):
-        source, left = 0, ends[half]
-        while left:
-            gap = max(free, key=lambda f: (f[1] + left <= f[2], f[1] == 0, f[2] - f[1]))
-            count = min(left, gap[2] - gap[1])
-            pieces.append((step, half, source, gap[0], gap[1], count))
-            gap[1] += count
-            source += count
-            left -= count
-    return groups, tuple(pieces)
-
-
-def packed_lane(pieces, step, half, lane):
+    for k in range(steps):
+        pieces += [
+            (k, 0, 0, k, 0, ends[0]),
+            (k, 1, 0, k, ends[0], first),
+            (k, 1, first, shared_group(steps, k), k % 2 * rest, rest),
+        ]
+    return steps + (steps + 1) // 2, tuple(pieces)
+
+
+def shared_group(steps, k):
+    return steps + k // 2
+
+
+def packed_lane(steps, pieces, step, half, lane):
     for s, h, source, group, goal, count in pieces:
         if (s, h) == (step, half) and source <= lane < source + count:
-            return group * LANES + goal + lane - source
+            return (group >= steps) * LANES + goal + lane - source
 
 
 @functools.cache
 def expansion_tables(steps, comps):
     dofs = NODES * comps
     pairs = component_pairs(comps)
-    groups, pieces = packing(steps, comps)
-    hessian = np.zeros((steps, groups * LANES, dofs * dofs), ml_dtypes.bfloat16)
-    gradient = np.zeros((steps * dofs, groups * LANES), ml_dtypes.bfloat16)
+    _, pieces = packing(steps, comps)
+    hessian = np.zeros((steps, 2 * LANES, dofs * dofs), ml_dtypes.bfloat16)
+    gradient = np.zeros((steps, dofs, 2 * LANES), ml_dtypes.bfloat16)
     for k in range(steps):
         for d in range(dofs):
             a, c = divmod(d, comps)
             half, at, _ = gradient_place(c)
-            gradient[k * dofs + d, packed_lane(pieces, k, half, at + a)] = 1
+            gradient[k, d, packed_lane(steps, pieces, k, half, at + a)] = 1
             for f in range(dofs):
                 b, e = divmod(f, comps)
                 quad = sum(((a >> n & 1) + (b >> n & 1)) * 3**n for n in range(3))
                 half, at, _ = pair_place(pairs.index((min(c, e), max(c, e))))
-                hessian[k, packed_lane(pieces, k, half, at + quad), d * dofs + f] = 1
+                hessian[k, packed_lane(steps, pieces, k, half, at + quad), d * dofs + f] = 1
     return hessian, gradient
 
 
@@ -343,7 +345,6 @@
     capacity, ready, last, table, gradient_table, hessian_hbm, gradient_hbm, total, wide, thin, sems
 ):
     steps, slots, _ = wide.shape
-    dofs = thin.shape[1]
     spaces = slots // capacity
     me = lax.axis_index("space")
     for distance in range(spaces):
@@ -351,18 +352,19 @@
         source = (me + spaces - distance) % spaces
         rows = pl.ds(pl.multiple_of(source * capacity, math.gcd(capacity, 8)), capacity)
         total[rows] = ready[here] + last[here]
-    parts = split(total[...])
     copies = []
+    parts = []
     for k in range(steps):
-        wide[k] = sum(jnp.dot(part, table[k], preferred_element_type=F32) for part in parts)
+        lanes = [slice(g * LANES, (g + 1) * LANES) for g in (k, shared_group(steps, k))]
+        parts.append(split(jnp.concatenate([total[:, cols] for cols in lanes], axis=1)))
+        wide[k] = sum(jnp.dot(part, table[k], preferred_element_type=F32) for part in parts[k])
         copies.append(pltpu.make_async_copy(wide.at[k], hessian_hbm.at[k], sems.at[k]))
         copies[-1].start()
-    gradient = sum(
-        lax.dot_general(gradient_table[...], part, (((1,), (1,)), ((), ())), preferred_element_type=F32)
-        for part in parts
-    )
     for k in range(steps):
-        thin[k] = gradient[k * dofs : (k + 1) * dofs]
+        thin[k] = sum(
+            lax.dot_general(gradient_table[k], part, (((1,), (1,)), ((), ())), preferred_element_type=F32)
+            for part in parts[k]
+        )
     copies.append(pltpu.make_async_copy(thin, gradient_hbm, sems.at[steps]))
     copies[-1].start()
     for copy in copies:

time: 18.3 us -> 18 us (0.984)
  Pallas kernels: 6.43 us -> 6.21 us
    pallas_call x1, Pallas kernels: 1.29 us -> 1.08 us  [per_device(): pl.pallas_call(functools.partial(expand_kernel, capacity), out_shape=[jax...]
where the time goes in v6:
time: 18 us; the launch traced here: 17.9 us
  Pallas kernels  6.21 us (34%)
  starting transfers between devices  5.63 us (31%)
  waiting for transfers between devices  5.27 us (29%)
  between operations  0.7 us (4%)
    ppermute x2, starting transfers between devices, exchange(): lax.ppermute(values, 'tm', route)  5.49 us
    pallas_call x1, Pallas kernels, per_device(): pl.pallas_call(functools.partial(moments_kernel, capacity, parts), in_spe...  4.84 us
    ppermute x2, waiting for transfers between devices, exchange(): lax.ppermute(values, 'tm', route)  3.98 us
    ppermute x2, waiting for transfers between devices, turned(): return lax.ppermute(values, 'space', route) if distance else values  1.29 us
    pallas_call x1, Pallas kernels, per_device(): pl.pallas_call(functools.partial(expand_kernel, capacity), out_shape=[jax...  1.08 us
  transfers between devices with their start and end apart: 4, of which 2 were waited for; matrix products, arithmetic and copies ran while one was open for 0% of the time, Pallas kernels for 2%

profile of v6, /device:TPU:24, one launch (start us, length us, event | category | flops | bytes accessed | tf_op | source)
XLA Modules:
  0.0 17.9 jit_solution(16053991485104055461)
XLA Ops:
  0.6 0.0 copy-start
  0.6 0.0 copy-start.1
  0.7 4.8 %moments.1 = (f32[64,384]{1,0:T(8,128)S(1)}, f32[64,384]{1,0:T(8,128)S(1)}, f32[48,384]{1,0:T(8,128)S(1)}, f32[48,384]{1,0:T(8,128)S(1)}) custom-call(bf16[2,3,64,4096]{3,2,1,0:T(8,128)(2,1)} %bitcast.5, bf16[2,64,4096]{2,1,0:T(8,128)(2,1)} %resid_hbm.1, s32[1,64]{1,0:T(1,128)} %bitcast.6, s32[1,64]{1,0:T(1,128)} %bitcast.7, f32[1,2]{1,0:T(1,128)} %bitcast.8, ...), custom_call_target="tpu_custom_call" | custom-call | tf_op jit(solution)/shard_map/moments/pallas_call | solution.py:386
  5.5 0.1 collective-permute-start.2
  5.6 1.5 %collective-permute-start = (f32[64,384]{1,0:T(8,128)S(1)}, f32[64,384]{1,0:T(8,128)S(1)}, u32[]{:S(2)}, u32[]{:S(2)}) collective-permute-start(f32[64,384]{1,0:T(8,128)S(1)} %get-tuple-element.9), channel_id=1, source_target_pairs={{0,2},{4,6},{8,10},{12,14},{16,18},{20,22},{24,26},{28,30},{2,0},{... | collective-permute-start | bytes 294920 | tf_op jit(solution)/shard_map/ppermute | solution.py:426
  7.1 0.0 collective-permute-done.2
  7.2 3.9 %collective-permute-start.3 = (f32[96,384]{1,0:T(8,128)S(1)}, f32[96,384]{1,0:T(8,128)S(1)}, u32[]{:S(2)}, u32[]{:S(2)}) collective-permute-start(f32[96,384]{1,0:T(8,128)S(1)} %pad_maximum_fusion), channel_id=1, source_target_pairs={{2,4},{6,8},{10,12},{14,16},{18,20},{22,24},{26,28},{4,2},{8,6},{1... | collective-permute-start | bytes 442376 | tf_op jit(solution)/shard_map/ppermute | solution.py:426
  11.1 0.0 collective-permute-done
  11.1 0.1 collective-permute-start.1
  11.2 1.3 %collective-permute-done.1.refs_1_ = f32[64,384]{1,0:T(8,128)S(1)} collective-permute-done((f32[64,384]{1,0:T(8,128)S(1)}, f32[64,384]{1,0:T(8,128)S(1)}, u32[]{:S(2)}, u32[]{:S(2)}) %collective-permute-start.1) | collective-permute-done | bytes 98336 | tf_op jit(solution)/shard_map/ppermute | solution.py:430
  12.5 0.3 %place.1.ready = f32[96,384]{1,0:T(8,128)S(1)} custom-call(f32[64,384]{1,0:T(8,128)S(1)} %add.3.refs_0_, f32[64,384]{1,0:T(8,128)S(1)} %collective-permute-done.1.refs_1_), custom_call_target="tpu_custom_call" | custom-call | tf_op jit(solution)/shard_map/place/pallas_call | solution.py:437
  12.8 4.0 %collective-permute-done.3.last = f32[96,384]{1,0:T(8,128)S(1)} collective-permute-done((f32[96,384]{1,0:T(8,128)S(1)}, f32[96,384]{1,0:T(8,128)S(1)}, u32[]{:S(2)}, u32[]{:S(2)}) %collective-permute-start.3) | collective-permute-done | bytes 147488 | tf_op jit(solution)/shard_map/ppermute | solution.py:426
  16.8 0.0 copy-done
  16.8 0.0 copy-done.1
  16.8 1.1 %expand.1 = (f32[2,96,576]{2,1,0:T(8,128)}, f32[2,24,96]{2,1,0:T(8,128)}) custom-call(f32[96,384]{1,0:T(8,128)S(1)} %place.1.ready, f32[96,384]{1,0:T(8,128)S(1)} %collective-permute-done.3.last, bf16[2,256,576]{2,1,0:T(8,128)(2,1)S(1)} %copy-done, bf16[2,24,256]{2,1,0:T(8,128)(2,1)S(1)} %copy-done.1), custom_call_target="tpu_custom_call" | custom-call | tf_op jit(solution)/shard_map/expand/pallas_call | solution.py:446
  (2 shorter events, 0.0 us)
Async XLA Ops:
  0.6 16.1 %copy-start = (bf16[2,256,576]{2,1,0:T(8,128)(2,1)S(1)}, bf16[2,256,576]{2,1,0:T(8,128)(2,1)}, u32[]{:S(2)}) copy-start(bf16[2,256,576]{2,1,0:T(8,128)(2,1)} %constant.10.clone.table) | copy-start | bytes 1769476
  0.6 16.1 %copy-start.1 = (bf16[2,24,256]{2,1,0:T(8,128)(2,1)S(1)}, bf16[2,24,256]{2,1,0:T(8,128)(2,1)}, u32[]{:S(2)}) copy-start(bf16[2,24,256]{2,1,0:T(8,128)(2,1)} %constant.11.clone.gradient_table) | copy-start | bytes 73732
  5.5 1.6 %collective-permute-start.2 = (f32[48,384]{1,0:T(8,128)S(1)}, f32[48,384]{1,0:T(8,128)S(1)}, u32[]{:S(2)}, u32[]{:S(2)}) collective-permute-start(f32[48,384]{1,0:T(8,128)S(1)} %get-tuple-element.11), channel_id=1, source_target_pairs={{0,1},{1,0},{2,3},{3,2},{4,5},{5,4},{6,7},{7,6},{8,9},{9,8},{10,11... | collective-permute-start | bytes 221192 | tf_op jit(solution)/shard_map/ppermute | solution.py:430
  5.6 5.5 %collective-permute-start = (f32[64,384]{1,0:T(8,128)S(1)}, f32[64,384]{1,0:T(8,128)S(1)}, u32[]{:S(2)}, u32[]{:S(2)}) collective-permute-start(f32[64,384]{1,0:T(8,128)S(1)} %get-tuple-element.9), channel_id=1, source_target_pairs={{0,2},{4,6},{8,10},{12,14},{16,18},{20,22},{24,26},{28,30},{2,0},{... | collective-permute-start | bytes 294920 | tf_op jit(solution)/shard_map/ppermute | solution.py:426
  7.2 9.6 %collective-permute-start.3 = (f32[96,384]{1,0:T(8,128)S(1)}, f32[96,384]{1,0:T(8,128)S(1)}, u32[]{:S(2)}, u32[]{:S(2)}) collective-permute-start(f32[96,384]{1,0:T(8,128)S(1)} %pad_maximum_fusion), channel_id=1, source_target_pairs={{2,4},{6,8},{10,12},{14,16},{18,20},{22,24},{26,28},{4,2},{8,6},{1... | collective-permute-start | bytes 442376 | tf_op jit(solution)/shard_map/ppermute | solution.py:426
  11.1 1.4 %collective-permute-start.1 = (f32[64,384]{1,0:T(8,128)S(1)}, f32[64,384]{1,0:T(8,128)S(1)}, u32[]{:S(2)}, u32[]{:S(2)}) collective-permute-start(f32[64,384]{1,0:T(8,128)S(1)} %add.3.refs_0_), channel_id=1, source_target_pairs={{0,1},{1,0},{2,3},{3,2},{4,5},{5,4},{6,7},{7,6},{8,9},{9,8},{10,11... | collective-permute-start | bytes 294920 | tf_op jit(solution)/shard_map/ppermute | solution.py:430

commit v7 on v6

--- a/solution.py
+++ b/solution.py
@@ -24,21 +24,21 @@
 
 
 @functools.cache
-def voxel_tables(voxels):
+def voxel_tables(voxels, comps):
     edge = round(voxels ** (1 / 3))
     at = (np.arange(edge) + 0.5) / edge
-    lines = np.stack([1 - at, at])
     quads = np.stack([(1 - at) ** 2, at * (1 - at), at * at])
-    shapes = np.einsum("ai,bj,ck->abcijk", lines, lines, lines).reshape(NODES, voxels)
+    odds = 2 * np.arange(edge) + 1 - edge
+    across = np.stack([odds[:, None] ** (m >> 1) * odds[None, :] ** (m & 1) for m in range(4)]).reshape(4, edge * edge)
     squares = np.einsum("ai,bj,ck->abcijk", quads, quads, quads).reshape(QUADS, voxels)
     scale = (1 + np.floor(128 * np.modf(np.arange(voxels) * 0.6180339887498949)[0]) / 128).reshape(1, voxels)
     squares = (squares / scale).astype(ml_dtypes.bfloat16)
-    high = shapes.astype(ml_dtypes.bfloat16)
-    low = (shapes - high.astype(np.float64)).astype(ml_dtypes.bfloat16)
-    table = np.zeros((LANES, voxels), ml_dtypes.bfloat16)
-    rows = np.concatenate([squares] * PER_HALF + [high, high, low, low])
-    table[: len(rows)] = rows
-    return np.ascontiguousarray(table.T), np.repeat(scale.astype(ml_dtypes.bfloat16), 16, axis=0)
+    table = np.zeros((voxels, LANES), ml_dtypes.bfloat16)
+    table[:, :GRAD_AT] = np.concatenate([squares] * PER_HALF).T
+    plane_table = np.zeros((edge * edge, LANES), ml_dtypes.bfloat16)
+    lines = np.concatenate([across] * (2 * ((comps + 1) // 2)))
+    plane_table[:, GRAD_AT : GRAD_AT + len(lines)] = lines.T
+    return table, plane_table, np.repeat(scale.astype(ml_dtypes.bfloat16), 16, axis=0)
 
 
 def voxel_parts(voxels, sixteenths):
@@ -84,7 +84,7 @@
 
 
 @functools.cache
-def expansion_tables(steps, comps):
+def expansion_tables(steps, comps, edge):
     dofs = NODES * comps
     pairs = component_pairs(comps)
     _, pieces = packing(steps, comps)
@@ -94,7 +94,13 @@
         for d in range(dofs):
             a, c = divmod(d, comps)
             half, at, _ = gradient_place(c)
-            gradient[k, d, packed_lane(steps, pieces, k, half, at + a)] = 1
+            for m in range(4):
+                weight = 0.25
+                for bit in range(2):
+                    if m >> bit & 1:
+                        weight *= (1 if a >> bit & 1 else -1) / edge
+                lane = packed_lane(steps, pieces, k, half, at + (a >> 2) * 4 + m)
+                gradient[k, d, lane] = weight
             for f in range(dofs):
                 b, e = divmod(f, comps)
                 quad = sum(((a >> n & 1) + (b >> n & 1)) * 3**n for n in range(3))
@@ -127,6 +133,7 @@
     owner_hbm,
     phase_hbm,
     table_hbm,
+    plane_table_hbm,
     scale_hbm,
     own_ref,
     send_a_ref,
@@ -141,10 +148,13 @@
         owner_ref,
         phase_ref,
         table,
+        plane_table,
         scale,
         products_a,
         products_b,
         limits,
+        running,
+        lines,
         sums,
         moments,
         small_sems,
@@ -152,7 +162,7 @@
     ) = refs
     steps, comps, bricks, voxels = grads.shape
     pairs = component_pairs(comps)
-    groups = len(pairs) + comps
+    groups = len(pairs)
     rows = steps * bricks
     plane = round(voxels ** (2 / 3))
     buffers = (products_a, products_b)
@@ -164,6 +174,7 @@
                 (owner_hbm, owner_ref),
                 (phase_hbm, phase_ref),
                 (scale_hbm, scale),
+                (plane_table_hbm, plane_table),
             ]
         )
     ]
@@ -188,29 +199,38 @@
     voxel = lax.broadcasted_iota(jnp.int16, (tall, plane), 1)
     zero = jnp.zeros((), BF16)
 
+    edge = voxels // plane
+
     def fill(k, products):
         start, width = parts[k]
         for b in range(0, bricks, tall):
             limit = (limits[b : b + tall] - start).astype(jnp.int16)
-            left = [[None] * comps for _ in range(steps)]
-            for p in range(0, width, plane):
-                cols = slice(start + p, start + p + plane)
-                valid = voxel + jnp.int16(p) < limit
-                scale_here = jnp.where(valid, scale[:tall, cols], zero)
-                for s in range(steps):
+            for s in range(steps):
+                total = [running[0, c, s, b : b + tall] for c in range(comps)] if k else None
+                ramp = [running[1, c, s, b : b + tall] for c in range(comps)] if k else None
+                for p in range(0, width, plane):
+                    cols = slice(start + p, start + p + plane)
+                    valid = voxel + jnp.int16(p) < limit
+                    scale_here = jnp.where(valid, scale[:tall, cols], zero)
                     resid_here = jnp.where(valid, resid[s, b : b + tall, cols], zero).astype(F32)
                     g = [grads[s, c, b : b + tall, cols] for c in range(comps)]
                     scaled = [x * scale_here for x in g]
-                    blocks = [scaled[c] * g[e] for c, e in pairs]
-                    for c in range(comps):
-                        exact = g[c].astype(F32) * resid_here
-                        if left[s][c] is not None:
-                            exact = exact + left[s][c]
-                        blocks.append(exact.astype(BF16))
-                        left[s][c] = exact - blocks[-1].astype(F32)
-                    for i, block in enumerate(blocks):
+                    for i, (c, e) in enumerate(pairs):
                         at = i * rows + s * bricks + b
-                        products[at : at + tall, p : p + plane] = block
+                        products[at : at + tall, p : p + plane] = scaled[c] * g[e]
+                    terms = [x.astype(F32) * resid_here for x in g]
+                    total = terms if total is None else [x + y for x, y in zip(total, terms)]
+                    ramp = total if ramp is None else [x + y for x, y in zip(ramp, total)]
+                for c in range(comps):
+                    if k + 1 < len(parts):
+                        running[0, c, s, b : b + tall] = total[c]
+                        running[1, c, s, b : b + tall] = ramp[c]
+                        continue
+                    falling = (ramp[c] - 0.5 * total[c]) * (1.0 / edge)
+                    for n, line in enumerate((falling, total[c] - falling)):
+                        at = ((n * comps + c) * steps + s) * bricks + b
+                        for m, part in enumerate(split(line)):
+                            lines[m, at : at + tall] = part
 
     def reduce(k, products):
         start, width = parts[k]
@@ -275,24 +295,25 @@
         fill(k, buffers[k % 2])
         reduce(k, buffers[k % 2])
 
-    doubled = (comps + 1) // 2 * NODES
+    line_sums = sum(
+        jnp.dot(lines[m], plane_table[...], preferred_element_type=F32) for m in range(2)
+    )
     for s in range(steps):
         halves = [jnp.zeros((bricks, LANES), F32) for _ in range(2)]
-        for i in range(groups):
+        for i in range(len(pairs)):
+            half, goal, span = pair_place(i)
             at = i * rows + s * bricks
-            block = sums[at : at + bricks]
-            if i < len(pairs):
-                half, goal, span = pair_place(i)
-                keep = (lane >= goal) & (lane < goal + span)
-            else:
-                half, goal, span = gradient_place(i - len(pairs))
-                keep = (lane >= goal) & (lane < goal + span)
-                keep |= (lane >= goal + doubled) & (lane < goal + doubled + span)
-            halves[half] = jnp.where(keep, block, halves[half])
+            keep = (lane >= goal) & (lane < goal + span)
+            halves[half] = jnp.where(keep, sums[at : at + bricks], halves[half])
+        for c in range(comps):
+            half, goal, span = gradient_place(c)
+            for n in range(2):
+                at = (n * comps + c) * rows + s * bricks
+                first = goal + n * span // 2
+                keep = (lane >= first) & (lane < first + span // 2)
+                halves[half] = jnp.where(keep, line_sums[at : at + bricks], halves[half])
         for half in range(2):
-            low = pltpu.roll(halves[half], LANES - doubled, 1)
-            whole = halves[half] + jnp.where(lane >= GRAD_AT, low, 0.0)
-            moments[s, :, half * LANES : (half + 1) * LANES] = whole
+            moments[s, :, half * LANES : (half + 1) * LANES] = halves[half]
 
     packed_groups, pieces = packing(steps, comps)
 
@@ -377,15 +398,16 @@
     places = lax.axis_size("tm")
     capacity = 3 * bricks // (2 * spaces)
     dofs = NODES * comps
-    groups = len(component_pairs(comps)) + comps
-    parts = voxel_parts(voxels, (2, 6, 8))
+    groups = len(component_pairs(comps))
+    plane = round(voxels ** (2 / 3))
+    parts = voxel_parts(voxels, (3, 6, 5, 2))
     widest = max(width for _, width in parts)
-    table, scale = voxel_tables(voxels)
+    table, plane_table, scale = voxel_tables(voxels, comps)
     block = (bricks, packing(steps, comps)[0] * LANES)
     in_hbm = pl.BlockSpec(memory_space=pltpu.HBM)
     own, send_a, *send_b = pl.pallas_call(
         functools.partial(moments_kernel, capacity, parts),
-        in_specs=[in_hbm] * 7,
+        in_specs=[in_hbm] * 8,
         out_shape=[pltpu.VMEM(block, F32)] * 2 + [pltpu.VMEM((capacity, block[1]), F32)] * spaces,
         scratch_shapes=[
             pltpu.VMEM((steps, comps, bricks, voxels), BF16),
@@ -394,13 +416,16 @@
             pltpu.VMEM((1, bricks), jnp.int32),
             pltpu.VMEM((1, steps), F32),
             pltpu.VMEM((voxels, LANES), BF16),
+            pltpu.VMEM((plane, LANES), BF16),
             pltpu.VMEM(scale.shape, BF16),
             pltpu.VMEM((groups * steps * bricks, widest), BF16),
             pltpu.VMEM((groups * steps * bricks, widest), BF16),
-            pltpu.VMEM((bricks, round(voxels ** (2 / 3))), jnp.int32),
+            pltpu.VMEM((bricks, plane), jnp.int32),
+            pltpu.VMEM((2, comps, steps, bricks, plane), F32),
+            pltpu.VMEM((2, 2 * comps * steps * bricks, plane), BF16),
             pltpu.VMEM((groups * steps * bricks, LANES), F32),
             pltpu.VMEM((steps, bricks, 2 * LANES), F32),
-            pltpu.SemaphoreType.DMA((4,)),
+            pltpu.SemaphoreType.DMA((5,)),
             pltpu.SemaphoreType.DMA((len(parts), 3)),
         ],
         compiler_params=pltpu.CompilerParams(vmem_limit_bytes=32 << 20),
@@ -415,6 +440,7 @@
                 owner.reshape(1, bricks),
                 phase.reshape(1, steps),
                 jnp.asarray(table),
+                jnp.asarray(plane_table),
                 jnp.asarray(scale),
             )
         )
@@ -440,7 +466,7 @@
         compiler_params=pltpu.CompilerParams(vmem_limit_bytes=8 << 20),
         name="place",
     )(*blocks)
-    hessian_table, gradient_table = (jnp.asarray(x) for x in expansion_tables(steps, comps))
+    hessian_table, gradient_table = (jnp.asarray(x) for x in expansion_tables(steps, comps, round(voxels ** (1 / 3))))
     wide = (steps, slots, dofs * dofs)
     thin = (steps, dofs, slots)
     hessian, gradient = pl.pallas_call(

time: 18 us -> 17.8 us (0.989)
  no operation moved by 1% of the time
where the time goes in v7:
time: 17.8 us; the launch traced here: 17.7 us
  Pallas kernels  6.04 us (34%)
  starting transfers between devices  5.64 us (32%)
  waiting for transfers between devices  5.27 us (30%)
  between operations  0.7 us (4%)
    ppermute x2, starting transfers between devices, exchange(): lax.ppermute(values, 'tm', route)  5.49 us
    pallas_call x1, Pallas kernels, per_device(): pl.pallas_call(functools.partial(moments_kernel, capacity, parts), in_spe...  4.67 us
    ppermute x2, waiting for transfers between devices, exchange(): lax.ppermute(values, 'tm', route)  3.98 us
    ppermute x2, waiting for transfers between devices, turned(): return lax.ppermute(values, 'space', route) if distance else values  1.29 us
    pallas_call x1, Pallas kernels, per_device(): pl.pallas_call(functools.partial(expand_kernel, capacity), out_shape=[jax...  1.08 us
  transfers between devices with their start and end apart: 4, of which 2 were waited for; matrix products, arithmetic and copies ran while one was open for 0% of the time, Pallas kernels for 2%

profile of v7, /device:TPU:24, one launch (start us, length us, event | category | flops | bytes accessed | tf_op | source)
XLA Modules:
  0.0 17.7 jit_solution(510355535409822210)
XLA Ops:
  0.6 0.0 copy-start
  0.6 0.0 copy-start.1
  0.7 4.7 %moments.1 = (f32[64,384]{1,0:T(8,128)S(1)}, f32[64,384]{1,0:T(8,128)S(1)}, f32[48,384]{1,0:T(8,128)S(1)}, f32[48,384]{1,0:T(8,128)S(1)}) custom-call(bf16[2,3,64,4096]{3,2,1,0:T(8,128)(2,1)} %bitcast.5, bf16[2,64,4096]{2,1,0:T(8,128)(2,1)} %resid_hbm.1, s32[1,64]{1,0:T(1,128)} %bitcast.6, s32[1,64]{1,0:T(1,128)} %bitcast.7, f32[1,2]{1,0:T(1,128)} %bitcast.8, ...), custom_call_target="tpu_custom_call" | custom-call | tf_op jit(solution)/shard_map/moments/pallas_call | solution.py:408
  5.3 0.1 collective-permute-start.2
  5.4 1.6 %collective-permute-start = (f32[64,384]{1,0:T(8,128)S(1)}, f32[64,384]{1,0:T(8,128)S(1)}, u32[]{:S(2)}, u32[]{:S(2)}) collective-permute-start(f32[64,384]{1,0:T(8,128)S(1)} %get-tuple-element.9), channel_id=1, source_target_pairs={{0,2},{4,6},{8,10},{12,14},{16,18},{20,22},{24,26},{28,30},{2,0},{... | collective-permute-start | bytes 294920 | tf_op jit(solution)/shard_map/ppermute | solution.py:452
  7.0 0.0 collective-permute-done.2
  7.0 3.9 %collective-permute-start.3 = (f32[96,384]{1,0:T(8,128)S(1)}, f32[96,384]{1,0:T(8,128)S(1)}, u32[]{:S(2)}, u32[]{:S(2)}) collective-permute-start(f32[96,384]{1,0:T(8,128)S(1)} %pad_maximum_fusion), channel_id=1, source_target_pairs={{2,4},{6,8},{10,12},{14,16},{18,20},{22,24},{26,28},{4,2},{8,6},{1... | collective-permute-start | bytes 442376 | tf_op jit(solution)/shard_map/ppermute | solution.py:452
  10.9 0.0 collective-permute-done
  11.0 0.1 collective-permute-start.1
  11.0 1.3 %collective-permute-done.1.refs_1_ = f32[64,384]{1,0:T(8,128)S(1)} collective-permute-done((f32[64,384]{1,0:T(8,128)S(1)}, f32[64,384]{1,0:T(8,128)S(1)}, u32[]{:S(2)}, u32[]{:S(2)}) %collective-permute-start.1) | collective-permute-done | bytes 98336 | tf_op jit(solution)/shard_map/ppermute | solution.py:456
  12.3 0.3 %place.1.ready = f32[96,384]{1,0:T(8,128)S(1)} custom-call(f32[64,384]{1,0:T(8,128)S(1)} %add.3.refs_0_, f32[64,384]{1,0:T(8,128)S(1)} %collective-permute-done.1.refs_1_), custom_call_target="tpu_custom_call" | custom-call | tf_op jit(solution)/shard_map/place/pallas_call | solution.py:463
  12.6 4.0 %collective-permute-done.3.last = f32[96,384]{1,0:T(8,128)S(1)} collective-permute-done((f32[96,384]{1,0:T(8,128)S(1)}, f32[96,384]{1,0:T(8,128)S(1)}, u32[]{:S(2)}, u32[]{:S(2)}) %collective-permute-start.3) | collective-permute-done | bytes 147488 | tf_op jit(solution)/shard_map/ppermute | solution.py:452
  16.6 0.0 copy-done
  16.6 0.0 copy-done.1
  16.6 1.1 %expand.1 = (f32[2,96,576]{2,1,0:T(8,128)}, f32[2,24,96]{2,1,0:T(8,128)}) custom-call(f32[96,384]{1,0:T(8,128)S(1)} %place.1.ready, f32[96,384]{1,0:T(8,128)S(1)} %collective-permute-done.3.last, bf16[2,256,576]{2,1,0:T(8,128)(2,1)S(1)} %copy-done, bf16[2,24,256]{2,1,0:T(8,128)(2,1)S(1)} %copy-done.1), custom_call_target="tpu_custom_call" | custom-call | tf_op jit(solution)/shard_map/expand/pallas_call | solution.py:472
  (2 shorter events, 0.0 us)
Async XLA Ops:
  0.6 16.0 %copy-start = (bf16[2,256,576]{2,1,0:T(8,128)(2,1)S(1)}, bf16[2,256,576]{2,1,0:T(8,128)(2,1)}, u32[]{:S(2)}) copy-start(bf16[2,256,576]{2,1,0:T(8,128)(2,1)} %constant.13.clone.table) | copy-start | bytes 1769476
  0.6 16.0 %copy-start.1 = (bf16[2,24,256]{2,1,0:T(8,128)(2,1)S(1)}, bf16[2,24,256]{2,1,0:T(8,128)(2,1)}, u32[]{:S(2)}) copy-start(bf16[2,24,256]{2,1,0:T(8,128)(2,1)} %constant.14.clone.gradient_table) | copy-start | bytes 73732
  5.3 1.6 %collective-permute-start.2 = (f32[48,384]{1,0:T(8,128)S(1)}, f32[48,384]{1,0:T(8,128)S(1)}, u32[]{:S(2)}, u32[]{:S(2)}) collective-permute-start(f32[48,384]{1,0:T(8,128)S(1)} %get-tuple-element.11), channel_id=1, source_target_pairs={{0,1},{1,0},{2,3},{3,2},{4,5},{5,4},{6,7},{7,6},{8,9},{9,8},{10,11... | collective-permute-start | bytes 221192 | tf_op jit(solution)/shard_map/ppermute | solution.py:456
  5.4 5.5 %collective-permute-start = (f32[64,384]{1,0:T(8,128)S(1)}, f32[64,384]{1,0:T(8,128)S(1)}, u32[]{:S(2)}, u32[]{:S(2)}) collective-permute-start(f32[64,384]{1,0:T(8,128)S(1)} %get-tuple-element.9), channel_id=1, source_target_pairs={{0,2},{4,6},{8,10},{12,14},{16,18},{20,22},{24,26},{28,30},{2,0},{... | collective-permute-start | bytes 294920 | tf_op jit(solution)/shard_map/ppermute | solution.py:452
  7.0 9.6 %collective-permute-start.3 = (f32[96,384]{1,0:T(8,128)S(1)}, f32[96,384]{1,0:T(8,128)S(1)}, u32[]{:S(2)}, u32[]{:S(2)}) collective-permute-start(f32[96,384]{1,0:T(8,128)S(1)} %pad_maximum_fusion), channel_id=1, source_target_pairs={{2,4},{6,8},{10,12},{14,16},{18,20},{22,24},{26,28},{4,2},{8,6},{1... | collective-permute-start | bytes 442376 | tf_op jit(solution)/shard_map/ppermute | solution.py:452
  11.0 1.4 %collective-permute-start.1 = (f32[64,384]{1,0:T(8,128)S(1)}, f32[64,384]{1,0:T(8,128)S(1)}, u32[]{:S(2)}, u32[]{:S(2)}) collective-permute-start(f32[64,384]{1,0:T(8,128)S(1)} %add.3.refs_0_), channel_id=1, source_target_pairs={{0,1},{1,0},{2,3},{3,2},{4,5},{5,4},{6,7},{7,6},{8,9},{9,8},{10,11... | collective-permute-start | bytes 294920 | tf_op jit(solution)/shard_map/ppermute | solution.py:456

commit v8 on v7

--- a/solution.py
+++ b/solution.py
@@ -331,11 +331,14 @@
 
     above = pack([coefficient(steps + k) if k < 2 else None for k in range(steps)])
     below = pack([coefficient(-1) if k == steps - 1 else None for k in range(steps)])
+    pick = jnp.concatenate(picks, axis=0)
     for group in range(packed_groups):
         cols = slice(group * LANES, (group + 1) * LANES)
         parts_b = split(jnp.where(odd, above[group], below[group]))
-        for pick, ref in zip(picks, send_b_refs):
-            ref[:, cols] = sum(jnp.dot(pick, part, preferred_element_type=F32) for part in parts_b)
+        both = jnp.dot(pick, jnp.concatenate(parts_b, axis=1), preferred_element_type=F32)
+        placed = both[:, :LANES] + both[:, LANES:]
+        for distance, ref in enumerate(send_b_refs):
+            ref[:, cols] = placed[distance * capacity : (distance + 1) * capacity]
         send_a_ref[:, cols] = jnp.where(odd, below[group], above[group])
     mine = pack([coefficient(k) for k in range(steps)])
     mine[-1] = jnp.where(lane == LANES - 1, destination, mine[-1])

time: 17.8 us -> 17.7 us (level)
  no operation moved by 1% of the time
where the time goes in v8:
time: 17.7 us; the launch traced here: 17.6 us
  Pallas kernels  5.91 us (33%)
  starting transfers between devices  5.63 us (32%)
  waiting for transfers between devices  5.29 us (30%)
  between operations  0.7 us (4%)
    ppermute x2, starting transfers between devices, exchange(): lax.ppermute(values, 'tm', route)  5.49 us
    pallas_call x1, Pallas kernels, per_device(): pl.pallas_call(functools.partial(moments_kernel, capacity, parts), in_spe...  4.55 us
    ppermute x2, waiting for transfers between devices, exchange(): lax.ppermute(values, 'tm', route)  4 us
    ppermute x2, waiting for transfers between devices, turned(): return lax.ppermute(values, 'space', route) if distance else values  1.29 us
    pallas_call x1, Pallas kernels, per_device(): pl.pallas_call(functools.partial(expand_kernel, capacity), out_shape=[jax...  1.08 us
  transfers between devices with their start and end apart: 4, of which 2 were waited for; matrix products, arithmetic and copies ran while one was open for 0% of the time, Pallas kernels for 2%

profile of v8, /device:TPU:24, one launch (start us, length us, event | category | flops | bytes accessed | tf_op | source)
XLA Modules:
  0.0 17.6 jit_solution(11664814570679657255)
XLA Ops:
  0.6 0.0 copy-start
  0.6 0.0 copy-start.1
  0.7 4.5 %moments.1 = (f32[64,384]{1,0:T(8,128)S(1)}, f32[64,384]{1,0:T(8,128)S(1)}, f32[48,384]{1,0:T(8,128)S(1)}, f32[48,384]{1,0:T(8,128)S(1)}) custom-call(bf16[2,3,64,4096]{3,2,1,0:T(8,128)(2,1)} %bitcast.5, bf16[2,64,4096]{2,1,0:T(8,128)(2,1)} %resid_hbm.1, s32[1,64]{1,0:T(1,128)} %bitcast.6, s32[1,64]{1,0:T(1,128)} %bitcast.7, f32[1,2]{1,0:T(1,128)} %bitcast.8, ...), custom_call_target="tpu_custom_call" | custom-call | tf_op jit(solution)/shard_map/moments/pallas_call | solution.py:411
  5.2 0.1 collective-permute-start.2
  5.3 1.6 %collective-permute-start = (f32[64,384]{1,0:T(8,128)S(1)}, f32[64,384]{1,0:T(8,128)S(1)}, u32[]{:S(2)}, u32[]{:S(2)}) collective-permute-start(f32[64,384]{1,0:T(8,128)S(1)} %get-tuple-element.9), channel_id=1, source_target_pairs={{0,2},{4,6},{8,10},{12,14},{16,18},{20,22},{24,26},{28,30},{2,0},{... | collective-permute-start | bytes 294920 | tf_op jit(solution)/shard_map/ppermute | solution.py:455
  6.9 0.0 collective-permute-done.2
  6.9 3.9 %collective-permute-start.3 = (f32[96,384]{1,0:T(8,128)S(1)}, f32[96,384]{1,0:T(8,128)S(1)}, u32[]{:S(2)}, u32[]{:S(2)}) collective-permute-start(f32[96,384]{1,0:T(8,128)S(1)} %pad_maximum_fusion), channel_id=1, source_target_pairs={{2,4},{6,8},{10,12},{14,16},{18,20},{22,24},{26,28},{4,2},{8,6},{1... | collective-permute-start | bytes 442376 | tf_op jit(solution)/shard_map/ppermute | solution.py:455
  10.8 0.0 collective-permute-done
  10.8 0.1 collective-permute-start.1
  10.9 1.3 %collective-permute-done.1.refs_1_ = f32[64,384]{1,0:T(8,128)S(1)} collective-permute-done((f32[64,384]{1,0:T(8,128)S(1)}, f32[64,384]{1,0:T(8,128)S(1)}, u32[]{:S(2)}, u32[]{:S(2)}) %collective-permute-start.1) | collective-permute-done | bytes 98336 | tf_op jit(solution)/shard_map/ppermute | solution.py:459
  12.2 0.3 %place.1.ready = f32[96,384]{1,0:T(8,128)S(1)} custom-call(f32[64,384]{1,0:T(8,128)S(1)} %add.3.refs_0_, f32[64,384]{1,0:T(8,128)S(1)} %collective-permute-done.1.refs_1_), custom_call_target="tpu_custom_call" | custom-call | tf_op jit(solution)/shard_map/place/pallas_call | solution.py:466
  12.5 4.0 %collective-permute-done.3.last = f32[96,384]{1,0:T(8,128)S(1)} collective-permute-done((f32[96,384]{1,0:T(8,128)S(1)}, f32[96,384]{1,0:T(8,128)S(1)}, u32[]{:S(2)}, u32[]{:S(2)}) %collective-permute-start.3) | collective-permute-done | bytes 147488 | tf_op jit(solution)/shard_map/ppermute | solution.py:455
  16.5 0.0 copy-done
  16.5 0.0 copy-done.1
  16.5 1.1 %expand.1 = (f32[2,96,576]{2,1,0:T(8,128)}, f32[2,24,96]{2,1,0:T(8,128)}) custom-call(f32[96,384]{1,0:T(8,128)S(1)} %place.1.ready, f32[96,384]{1,0:T(8,128)S(1)} %collective-permute-done.3.last, bf16[2,256,576]{2,1,0:T(8,128)(2,1)S(1)} %copy-done, bf16[2,24,256]{2,1,0:T(8,128)(2,1)S(1)} %copy-done.1), custom_call_target="tpu_custom_call" | custom-call | tf_op jit(solution)/shard_map/expand/pallas_call | solution.py:475
  (2 shorter events, 0.0 us)
Async XLA Ops:
  0.6 15.9 %copy-start = (bf16[2,256,576]{2,1,0:T(8,128)(2,1)S(1)}, bf16[2,256,576]{2,1,0:T(8,128)(2,1)}, u32[]{:S(2)}) copy-start(bf16[2,256,576]{2,1,0:T(8,128)(2,1)} %constant.13.clone.table) | copy-start | bytes 1769476
  0.6 15.8 %copy-start.1 = (bf16[2,24,256]{2,1,0:T(8,128)(2,1)S(1)}, bf16[2,24,256]{2,1,0:T(8,128)(2,1)}, u32[]{:S(2)}) copy-start(bf16[2,24,256]{2,1,0:T(8,128)(2,1)} %constant.14.clone.gradient_table) | copy-start | bytes 73732
  5.2 1.6 %collective-permute-start.2 = (f32[48,384]{1,0:T(8,128)S(1)}, f32[48,384]{1,0:T(8,128)S(1)}, u32[]{:S(2)}, u32[]{:S(2)}) collective-permute-start(f32[48,384]{1,0:T(8,128)S(1)} %get-tuple-element.11), channel_id=1, source_target_pairs={{0,1},{1,0},{2,3},{3,2},{4,5},{5,4},{6,7},{7,6},{8,9},{9,8},{10,11... | collective-permute-start | bytes 221192 | tf_op jit(solution)/shard_map/ppermute | solution.py:459
  5.3 5.5 %collective-permute-start = (f32[64,384]{1,0:T(8,128)S(1)}, f32[64,384]{1,0:T(8,128)S(1)}, u32[]{:S(2)}, u32[]{:S(2)}) collective-permute-start(f32[64,384]{1,0:T(8,128)S(1)} %get-tuple-element.9), channel_id=1, source_target_pairs={{0,2},{4,6},{8,10},{12,14},{16,18},{20,22},{24,26},{28,30},{2,0},{... | collective-permute-start | bytes 294920 | tf_op jit(solution)/shard_map/ppermute | solution.py:455
  6.9 9.6 %collective-permute-start.3 = (f32[96,384]{1,0:T(8,128)S(1)}, f32[96,384]{1,0:T(8,128)S(1)}, u32[]{:S(2)}, u32[]{:S(2)}) collective-permute-start(f32[96,384]{1,0:T(8,128)S(1)} %pad_maximum_fusion), channel_id=1, source_target_pairs={{2,4},{6,8},{10,12},{14,16},{18,20},{22,24},{26,28},{4,2},{8,6},{1... | collective-permute-start | bytes 442376 | tf_op jit(solution)/shard_map/ppermute | solution.py:455
  10.8 1.4 %collective-permute-start.1 = (f32[64,384]{1,0:T(8,128)S(1)}, f32[64,384]{1,0:T(8,128)S(1)}, u32[]{:S(2)}, u32[]{:S(2)}) collective-permute-start(f32[64,384]{1,0:T(8,128)S(1)} %add.3.refs_0_), channel_id=1, source_target_pairs={{0,1},{1,0},{2,3},{3,2},{4,5},{5,4},{6,7},{7,6},{8,9},{9,8},{10,11... | collective-permute-start | bytes 294920 | tf_op jit(solution)/shard_map/ppermute | solution.py:459
